TPU v7x, 128 devices: a whole 4x4x4 slice. The times are simulated.
128 devices in a mesh: wide: 32 (over x_lo, z, y), tp: 4 (over x_hi, core).
Axes of the slice: x: 4 (x_hi: 2, x_lo: 2; x = x_hi * 2 + x_lo), y: 4, z: 4, core: 2. Of those that a mesh axis runs over, the one named last changes fastest.
Arguments:
- cache: bfloat16 [1024, 256, 576], P('wide'), may hold values from -4 to 4
- queries: bfloat16 [32, 32, 3, 64, 576], P('wide', None, None, 'tp'), may hold values from -28 to 28
- new_latent: bfloat16 [32, 32, 3, 576], P('wide'), may hold values from -4 to 4
- cache_len: int32 [1024], replicated, may hold values from 1 to 256, 163840 in all
- owner: int32 [1024], replicated, may hold values from 0 to 31, as said below
- moe_tokens: bfloat16 [3, 1024, 7168], P(None, 'wide'), may hold values from -6 to 6
- expert_ids: int32 [3, 1024, 8], P(None, 'wide'), may hold values from 0 to 31, all different within a row; in each aligned block of 32 rows (0 to 31, 32 to 63, ..., all dimensions but the last counted through in order) at most 9 rows name the same one
- gate_weights: float32 [3, 1024, 8], P(None, 'wide'), may hold values from 0.05 to 0.5
- w_gate: bfloat16 [32, 7168, 1024], P('wide', None, 'tp'), may hold values from -0.0625 to 0.0625
- w_up: bfloat16 [32, 7168, 1024], P('wide', None, 'tp'), may hold values from -0.0625 to 0.0625
- w_down: bfloat16 [32, 1024, 7168], P('wide', 'tp'), may hold values from -0.1875 to 0.1875
Outputs:
- attn_out: bfloat16 [32, 32, 3, 64, 512], P('wide', None, None, 'tp')
- moe_out: bfloat16 [3, 1024, 7168], P(None, 'wide', 'tp')
Inputs may be any that keep to these rules, and one draw needn't show every extreme that they name: Requests 32 * g to 32 * g + 31 belong to prefill group g. No decode owner serves more than 1 request of one group, and some owner serves exactly 1 from every group.
All inputs are finite; a program needn't handle non-finite values.
Results may differ from a plain program's by a relative error of at most 0.017.
Values may be sent and summed in bfloat16 or wider, within the bound.
A program may use at most 192 MiB of HBM per device.

v0:
```python
import jax
import jax.numpy as jnp
from jax import lax
from jax.sharding import PartitionSpec as P

KVL = 512


score_scale = 192.0 ** (-0.5)
masked_score = -1e30


def latent_attend(latents, queries_in, new_keys, lengths):
    positions = jnp.arange(latents.shape[1], dtype=jnp.int32)
    cache_valid = (positions[None, :] < lengths[:, None])[:, None, None, :]
    step_ids = jnp.arange(queries_in.shape[1], dtype=jnp.int32)
    fresh_valid = (step_ids[None, :] <= step_ids[:, None])[None, :, None, :]
    cache_scores = (
        jnp.einsum("gshl,gcl->gshc", queries_in, latents, preferred_element_type=jnp.float32)
        * score_scale
    )
    fresh_scores = (
        jnp.einsum("gshl,gtl->gsht", queries_in, new_keys, preferred_element_type=jnp.float32)
        * score_scale
    )
    cache_scores = jnp.where(cache_valid, cache_scores, masked_score)
    fresh_scores = jnp.where(fresh_valid, fresh_scores, masked_score)
    top_score = jnp.maximum(jnp.max(cache_scores, -1), jnp.max(fresh_scores, -1))[..., None]
    cache_weights = jnp.where(cache_valid, jnp.exp(cache_scores - top_score), 0.0)
    fresh_weights = jnp.where(fresh_valid, jnp.exp(fresh_scores - top_score), 0.0)
    totals = jnp.sum(cache_weights, -1) + jnp.sum(fresh_weights, -1)
    context = jnp.einsum(
        "gshc,gck->gshk",
        cache_weights.astype(jnp.bfloat16),
        latents[..., :KVL],
        preferred_element_type=jnp.float32,
    )
    context = context + jnp.einsum(
        "gsht,gtk->gshk",
        fresh_weights.astype(jnp.bfloat16),
        new_keys[..., :KVL],
        preferred_element_type=jnp.float32,
    )
    return context / totals[..., None]


def shards(
    cache,
    queries,
    new_latent,
    cache_len,
    owner,
    moe_tokens,
    expert_ids,
    gate_weights,
    w_gate,
    w_up,
    w_down,
):
    wide_count = lax.axis_size("wide")
    wide_index = lax.axis_index("wide")
    group_reqs = cache.shape[0]
    pair_slots = max(1, group_reqs // wide_count)
    owner_grid = owner.reshape(wide_count, group_reqs)
    length_grid = cache_len.reshape(wide_count, group_reqs)
    owner_ids = jnp.arange(wide_count, dtype=jnp.int32)
    owner_hits = (owner_grid[:, :, None] == owner_ids[None, None, :]).astype(jnp.int32)
    earlier = jnp.cumsum(owner_hits, axis=1) - owner_hits
    slot_rank = jnp.sum(earlier * owner_hits, axis=2)
    pair_ids = jnp.arange(pair_slots, dtype=jnp.int32)
    mine_owner = lax.dynamic_index_in_dim(owner_grid, wide_index, 0, keepdims=False)
    mine_rank = lax.dynamic_index_in_dim(slot_rank, wide_index, 0, keepdims=False)
    sender = (
        (mine_owner[None, None, :] == owner_ids[:, None, None])
        & (mine_rank[None, None, :] == pair_ids[None, :, None])
    ).astype(jnp.bfloat16)
    arriving = (owner_grid == wide_index)[:, None, :] & (
        slot_rank[:, None, :] == pair_ids[None, :, None]
    )
    slot_length = jnp.sum(jnp.where(arriving, length_grid[:, None, :], 0), axis=2)
    slot_filled = jnp.any(arriving, axis=2)
    send_cache = jnp.einsum(
        "wpj,jcl->wpcl", sender, cache, preferred_element_type=jnp.float32
    ).astype(jnp.bfloat16)
    got_cache = lax.all_to_all(send_cache, "wide", split_axis=0, concat_axis=0, tiled=True)
    slot_total = wide_count * pair_slots
    context = latent_attend(
        got_cache.reshape((slot_total,) + got_cache.shape[2:]),
        queries[0],
        new_latent[0],
        slot_length.reshape(slot_total),
    )
    context = jnp.where(slot_filled.reshape(slot_total)[:, None, None, None], context, 0.0).astype(
        jnp.bfloat16
    )
    attn_out = context.reshape((1, slot_total) + context.shape[1:])
    step_count = moe_tokens.shape[0]
    top_count = expert_ids.shape[2]
    model_width = moe_tokens.shape[2]
    route_cap = min(group_reqs, group_reqs * top_count // wide_count + 1)
    expert_range = jnp.arange(wide_count, dtype=jnp.int32)
    cap_range = jnp.arange(route_cap, dtype=jnp.int32)
    outputs = []
    for decode_step in range(step_count):
        tokens_now = moe_tokens[decode_step]
        flat_ids = expert_ids[decode_step].reshape(-1)
        route_hits = (flat_ids[:, None] == expert_range[None, :]).astype(jnp.int32)
        before = jnp.cumsum(route_hits, axis=0) - route_hits
        route_rank = jnp.sum(before * route_hits, axis=1)
        placed = (route_hits.T[:, None, :] == 1) & (
            route_rank[None, None, :] == cap_range[None, :, None]
        )
        placed_tokens = placed.reshape(wide_count, route_cap, group_reqs, top_count)
        token_pick = jnp.any(placed_tokens, axis=3).astype(jnp.bfloat16)
        mix_weight = jnp.sum(
            jnp.where(placed_tokens, gate_weights[decode_step][None, None, :, :], 0.0), axis=3
        )
        outgoing = jnp.einsum(
            "ecj,jd->ecd", token_pick, tokens_now, preferred_element_type=jnp.float32
        ).astype(jnp.bfloat16)
        rows_in = lax.all_to_all(outgoing, "wide", split_axis=0, concat_axis=0, tiled=True)
        rows_flat = rows_in.reshape(wide_count * route_cap, model_width)
        gate_value = jnp.dot(rows_flat, w_gate[0], preferred_element_type=jnp.float32)
        up_value = jnp.dot(rows_flat, w_up[0], preferred_element_type=jnp.float32)
        hidden = (jax.nn.silu(gate_value) * up_value).astype(jnp.bfloat16)
        partial_out = jnp.dot(hidden, w_down[0], preferred_element_type=jnp.float32)
        summed = lax.psum_scatter(
            partial_out.astype(jnp.bfloat16), "tp", scatter_dimension=1, tiled=True
        )
        returned = lax.all_to_all(
            summed.reshape(wide_count, route_cap, summed.shape[1]),
            "wide",
            split_axis=0,
            concat_axis=0,
            tiled=True,
        )
        mixed_rows = jnp.einsum("ecj,ecd->jd", mix_weight, returned.astype(jnp.float32))
        outputs.append(mixed_rows.astype(jnp.bfloat16))
    moe_out = jnp.stack(outputs)
    return (attn_out, moe_out)


def solution(mesh):
    in_specs = (
        P("wide", None, None),
        P("wide", None, None, "tp", None),
        P("wide", None, None, None),
        P(),
        P(),
        P(None, "wide", None),
        P(None, "wide", None),
        P(None, "wide", None),
        P("wide", None, "tp"),
        P("wide", None, "tp"),
        P("wide", "tp", None),
    )
    out_specs = (P("wide", None, None, "tp", None), P(None, "wide", "tp"))
    return jax.shard_map(shards, mesh=mesh, in_specs=in_specs, out_specs=out_specs, check_vma=False)
```

profile of v0, /device:TPU:15, one launch (start us, length us, event | category | flops | bytes accessed | tf_op | source)
XLA Modules:
  0.0 649.3 jit_solution(3846910385462724484)
XLA Ops:
  7.2 0.9 slice_bitcast_fusion.9
  8.4 0.6 reduce-window.26
  9.5 0.4 and_reduce_fusion
  9.9 2.2 convolution_convert_fusion.1
  12.1 2.6 copy.135
  14.7 91.3 %all_to_all.35 = bf16[32,9,7168]{2,1,0:T(8,128)(2,1)} all-to-all(bf16[32,9,7168]{2,1,0:T(8,128)(2,1)S(1)} %copy.135), channel_id=1, replica_groups=mesh['wide'=32,'tp'=4] {'wide'}, dimensions={0} | all-to-all | bytes 8257536 | tf_op jit(solution)/shard_map/all_to_all | solution.py:121
  106.1 6.3 reshape.381
  112.4 4.7 fusion.16
  117.0 0.9 copy-done.12
  117.9 1.3 fusion.52
  119.2 0.7 copy-done.1
  120.0 3.3 convolution_convert_fusion
  123.5 0.6 reduce-window.24
  124.7 0.4 and_reduce_fusion.1
  125.1 1.2 convolution_convert_fusion.3
  126.3 5.7 copy.127
  131.9 7.0 %all-to-all-start.3 = ((bf16[32,9,7168]{2,1,0:T(8,128)(2,1)}), bf16[32,9,7168]{2,1,0:T(8,128)(2,1)}, u32[]{:S(2)}, u32[]{:S(2)}) async-start(bf16[32,9,7168]{2,1,0:T(8,128)(2,1)} %copy.127), calls=%async_computation.4 | async-start | bytes 14680064 | tf_op jit(solution)/shard_map/all_to_all | solution.py:121
  139.4 0.6 reduce-window.20
  140.5 106.0 %all-to-all-done.3 = bf16[32,9,7168]{2,1,0:T(8,128)(2,1)} async-done(((bf16[32,9,7168]{2,1,0:T(8,128)(2,1)}), bf16[32,9,7168]{2,1,0:T(8,128)(2,1)}, u32[]{:S(2)}, u32[]{:S(2)}) %all-to-all-start.3) | async-done | bytes 4128800 | tf_op jit(solution)/shard_map/all_to_all | solution.py:121
  246.5 6.3 reshape.378
  252.8 4.7 fusion.18
  257.5 0.9 copy-done.13
  258.4 1.3 fusion.55
  259.7 0.7 copy-done.2
  260.4 3.2 convolution_convert_fusion.2
  263.6 0.4 and_reduce_fusion.2
  264.0 1.2 convolution_convert_fusion.5
  265.2 5.5 copy.119
  270.7 13.8 %all-to-all-start.1 = ((bf16[32,9,7168]{2,1,0:T(8,128)(2,1)}), bf16[32,9,7168]{2,1,0:T(8,128)(2,1)}, u32[]{:S(2)}, u32[]{:S(2)}) async-start(bf16[32,9,7168]{2,1,0:T(8,128)(2,1)} %copy.119), calls=%async_computation.1 | async-start | bytes 14680064 | tf_op jit(solution)/shard_map/all_to_all | solution.py:121
  284.7 1.0 fusion.118
  286.0 13.5 %convert_bitcast_fusion = bf16[32,1,256,576]{2,0,3,1:T(8,128)(2,1)} fusion(bf16[32,256,576]{1,2,0:T(8,128)(2,1)} %param.11, s32[32]{0:T(128)S(1)} %dynamic-slice_bitcast_fusion, pred[32]{0:T(512)(128)(4,1)S(1)} %fusion.112), kind=kOutput, calls=%fused_computation.4 | convolution fusion | flops 306710528 | bytes 18874528 | tf_op jit(solution)/shard_map/wpj,jcl->wpcl/dot_general | solution.py:82
  299.4 13.1 %copy.111 = bf16[32,1,256,576]{2,3,1,0:T(8,128)(2,1)} copy(bf16[32,1,256,576]{2,0,3,1:T(8,128)(2,1)} %convert_bitcast_fusion) | data formatting | bytes 18874368 | tf_op jit(solution)/shard_map/convert_element_type | solution.py:84
  312.6 76.8 %all-to-all-done.1 = bf16[32,9,7168]{2,1,0:T(8,128)(2,1)} async-done(((bf16[32,9,7168]{2,1,0:T(8,128)(2,1)}), bf16[32,9,7168]{2,1,0:T(8,128)(2,1)}, u32[]{:S(2)}, u32[]{:S(2)}) %all-to-all-start.1) | async-done | bytes 4128800 | tf_op jit(solution)/shard_map/all_to_all | solution.py:121
  389.3 11.6 %all-to-all-start = ((bf16[32,1,256,576]{2,3,1,0:T(8,128)(2,1)}), bf16[32,1,256,576]{2,3,1,0:T(8,128)(2,1)}, u32[]{:S(2)}, u32[]{:S(2)}) async-start(bf16[32,1,256,576]{2,3,1,0:T(8,128)(2,1)} %copy.111), calls=%async_computation | async-start | bytes 18874368 | tf_op jit(solution)/shard_map/all_to_all | solution.py:85
  401.0 6.4 reshape.375
  407.3 4.7 fusion.20
  412.0 0.9 copy-done.14
  412.9 1.3 fusion.58
  414.2 0.7 copy-done.3
  415.0 3.2 convolution_convert_fusion.4
  418.4 0.5 copy-done.11
  419.3 2.5 reshape.382
  421.8 116.3 %all-to-all-done = bf16[32,1,256,576]{2,3,1,0:T(8,128)(2,1)} async-done(((bf16[32,1,256,576]{2,3,1,0:T(8,128)(2,1)}), bf16[32,1,256,576]{2,3,1,0:T(8,128)(2,1)}, u32[]{:S(2)}, u32[]{:S(2)}) %all-to-all-start) | async-done | bytes 9437216 | tf_op jit(solution)/shard_map/all_to_all | solution.py:85
  538.1 18.1 %all-to-all-start.6 = ((bf16[32,9,1792]{2,1,0:T(8,128)(2,1)}), bf16[32,9,1792]{2,1,0:T(8,128)(2,1)}, u32[]{:S(2)}, u32[]{:S(2)}) async-start(bf16[32,9,1792]{2,1,0:T(8,128)(2,1)} %reshape.382), calls=%async_computation.9 | async-start | bytes 3670016 | tf_op jit(solution)/shard_map/all_to_all | solution.py:130
  556.2 0.4 fusion.42
  556.6 0.4 fusion.41
  557.1 0.4 fusion.40
  557.6 2.2 fusion.119
  559.9 2.5 reshape.379
  562.4 15.0 %all-to-all-done.6 = bf16[32,9,1792]{2,1,0:T(8,128)(2,1)} async-done(((bf16[32,9,1792]{2,1,0:T(8,128)(2,1)}), bf16[32,9,1792]{2,1,0:T(8,128)(2,1)}, u32[]{:S(2)}, u32[]{:S(2)}) %all-to-all-start.6) | async-done | bytes 1032224 | tf_op jit(solution)/shard_map/all_to_all | solution.py:130
  577.4 9.0 %all-to-all-start.4 = ((bf16[32,9,1792]{2,1,0:T(8,128)(2,1)}), bf16[32,9,1792]{2,1,0:T(8,128)(2,1)}, u32[]{:S(2)}, u32[]{:S(2)}) async-start(bf16[32,9,1792]{2,1,0:T(8,128)(2,1)} %reshape.379), calls=%async_computation.6 | async-start | bytes 3670016 | tf_op jit(solution)/shard_map/all_to_all | solution.py:130
  586.4 5.5 bitcast_reduce_fusion
  591.9 0.7 fusion.38
  592.6 7.6 %fusion.4 = f32[32,3,16,512]{3,2,1,0:T(8,128)} fusion(bf16[32,256,576]{1,2,0:T(8,128)(2,1)} %bitcast.4, f32[32,256,3,16]{1,3,2,0:T(8,128)S(1)} %get-tuple-element.14, f32[32,3,16]{2,1,0:T(4,128)S(1)} %max.7, pred[32,256]{1,0:T(8,128)(4,1)S(1)} %iota_compare_fusion.14), kind=kOutput, calls=%fused_computation.12 | convolution fusion | flops 403832832 | bytes 13121536 | tf_op jit(solution)/shard_map/gshc,gck->gshk/dot_general | solution.py:32
  600.1 2.5 reshape.376
  602.6 6.3 all-to-all-done.4
  608.9 8.1 %all-to-all-start.2 = ((bf16[32,9,1792]{2,1,0:T(8,128)(2,1)}), bf16[32,9,1792]{2,1,0:T(8,128)(2,1)}, u32[]{:S(2)}, u32[]{:S(2)}) async-start(bf16[32,9,1792]{2,1,0:T(8,128)(2,1)} %reshape.376), calls=%async_computation.3 | async-start | bytes 3670016 | tf_op jit(solution)/shard_map/all_to_all | solution.py:130
  617.0 0.2 fusion.91
  617.2 4.0 fusion.33
  621.3 2.0 fusion.25
  623.2 2.0 fusion.26
  625.2 14.6 %all-to-all-done.2 = bf16[32,9,1792]{2,1,0:T(8,128)(2,1)} async-done(((bf16[32,9,1792]{2,1,0:T(8,128)(2,1)}), bf16[32,9,1792]{2,1,0:T(8,128)(2,1)}, u32[]{:S(2)}, u32[]{:S(2)}) %all-to-all-start.2) | async-done | bytes 1032224 | tf_op jit(solution)/shard_map/all_to_all | solution.py:130
  639.8 2.0 fusion.27
  641.8 0.8 pad_maximum_fusion
  (84 shorter events, 3.8 us)
Async XLA Ops:
  7.2 550.4 %copy-start = (bf16[1,32,3,16,576]{4,3,2,1,0:T(8,128)(2,1)S(1)}, bf16[1,32,3,16,576]{4,3,2,1,0:T(8,128)(2,1)}, u32[]{:S(2)}) copy-start(bf16[1,32,3,16,576]{4,3,2,1,0:T(8,128)(2,1)} %param.12) | copy-start | bytes 5308420
  7.2 412.1 %reduce-scatter.8.cloned.1.call-start = ((), (), s32[]{:S(2)}) async-start(), calls=%async_computation.12 | async-start | bytes 5160960 | tf_op jit(solution)/shard_map/reduce_scatter | solution.py:127
  112.4 4.7 copy-start.4
  112.4 5.6 copy-start.12
  117.9 2.0 copy-start.1
  123.3 1.8 copy-start.7
  131.9 114.6 %all-to-all-start.3 = ((bf16[32,9,7168]{2,1,0:T(8,128)(2,1)}), bf16[32,9,7168]{2,1,0:T(8,128)(2,1)}, u32[]{:S(2)}, u32[]{:S(2)}) async-start(bf16[32,9,7168]{2,1,0:T(8,128)(2,1)} %copy.127), calls=%async_computation.4 | async-start | bytes 14680064 | tf_op jit(solution)/shard_map/all_to_all | solution.py:121
  138.9 421.0 %reduce-scatter.6.cloned.1.call-start = ((), (), s32[]{:S(2)}) async-start(), calls=%async_computation.11 | async-start | bytes 5160960 | tf_op jit(solution)/shard_map/reduce_scatter | solution.py:127
  252.8 4.7 copy-start.5
  252.8 5.6 copy-start.13
  258.4 2.0 copy-start.2
  270.7 13.8 %copy-start.9 = (s32[1024]{0:T(1024)S(1)}, s32[1024]{0:T(1024)}, u32[]{:S(2)}) copy-start(s32[1024]{0:T(1024)} %param.15) | copy-start | bytes 12292
  270.7 118.6 %all-to-all-start.1 = ((bf16[32,9,7168]{2,1,0:T(8,128)(2,1)}), bf16[32,9,7168]{2,1,0:T(8,128)(2,1)}, u32[]{:S(2)}, u32[]{:S(2)}) async-start(bf16[32,9,7168]{2,1,0:T(8,128)(2,1)} %copy.119), calls=%async_computation.1 | async-start | bytes 14680064 | tf_op jit(solution)/shard_map/all_to_all | solution.py:121
  389.3 148.8 %all-to-all-start = ((bf16[32,1,256,576]{2,3,1,0:T(8,128)(2,1)}), bf16[32,1,256,576]{2,3,1,0:T(8,128)(2,1)}, u32[]{:S(2)}, u32[]{:S(2)}) async-start(bf16[32,1,256,576]{2,3,1,0:T(8,128)(2,1)} %copy.111), calls=%async_computation | async-start | bytes 18874368 | tf_op jit(solution)/shard_map/all_to_all | solution.py:85
  400.9 199.2 %reduce-scatter.4.cloned.1.call-start = ((), (), s32[]{:S(2)}) async-start(), calls=%async_computation.10 | async-start | bytes 5160960 | tf_op jit(solution)/shard_map/reduce_scatter | solution.py:127
  407.3 4.7 copy-start.6
  407.3 5.6 copy-start.14
  412.9 2.0 copy-start.3
  418.2 0.7 copy-start.11
  418.2 0.9 copy-start.8
  418.2 1.1 copy-start.10
  538.1 39.3 %all-to-all-start.6 = ((bf16[32,9,1792]{2,1,0:T(8,128)(2,1)}), bf16[32,9,1792]{2,1,0:T(8,128)(2,1)}, u32[]{:S(2)}, u32[]{:S(2)}) async-start(bf16[32,9,1792]{2,1,0:T(8,128)(2,1)} %reshape.382), calls=%async_computation.9 | async-start | bytes 3670016 | tf_op jit(solution)/shard_map/all_to_all | solution.py:130
  577.4 31.5 %all-to-all-start.4 = ((bf16[32,9,1792]{2,1,0:T(8,128)(2,1)}), bf16[32,9,1792]{2,1,0:T(8,128)(2,1)}, u32[]{:S(2)}, u32[]{:S(2)}) async-start(bf16[32,9,1792]{2,1,0:T(8,128)(2,1)} %reshape.379), calls=%async_computation.6 | async-start | bytes 3670016 | tf_op jit(solution)/shard_map/all_to_all | solution.py:130
  608.9 30.9 %all-to-all-start.2 = ((bf16[32,9,1792]{2,1,0:T(8,128)(2,1)}), bf16[32,9,1792]{2,1,0:T(8,128)(2,1)}, u32[]{:S(2)}, u32[]{:S(2)}) async-start(bf16[32,9,1792]{2,1,0:T(8,128)(2,1)} %reshape.376), calls=%async_computation.3 | async-start | bytes 3670016 | tf_op jit(solution)/shard_map/all_to_all | solution.py:130
Sparse Core Ops, SparseCore 0:
  123.4 72.7 reduce-scatter.7
  263.7 80.6 reduce-scatter.5
  418.3 75.5 reduce-scatter.3
where the time goes:
time: 658 us; the launch traced here: 649 us
  waiting for transfers between devices  335 us (51%)
  blocking collectives  91.3 us (14%)
  matrix products  70.8 us (11%)
  starting transfers between devices  67.8 us (10%)
  local copies, waits for them, and re-layouts  62 us (9%)
  between operations  14.4 us (2%)
  other arithmetic  7.87 us (1%)
    all_to_all x2, waiting for transfers between devices, shards(): lax.all_to_all(outgoing, 'wide', split_axis=0, concat_axis=0, tiled=True)  183 us
    all_to_all x1, waiting for transfers between devices, shards(): lax.all_to_all(send_cache, 'wide', split_axis=0, concat_axis=0, tiled=True)  116 us
    all_to_all x1, blocking collectives, shards(): lax.all_to_all(outgoing, 'wide', split_axis=0, concat_axis=0, tiled=True)  91.3 us
    all_to_all x3, waiting for transfers between devices, shards(): lax.all_to_all(summed.reshape(wide_count, route_cap, summed.shape[1]), 'w...  35.9 us
    all_to_all x3, starting transfers between devices, shards(): lax.all_to_all(summed.reshape(wide_count, route_cap, summed.shape[1]), 'w...  35.1 us
    all_to_all x2, starting transfers between devices, shards(): lax.all_to_all(outgoing, 'wide', split_axis=0, concat_axis=0, tiled=True)  20.8 us
    reshape x3, local copies, waits for them, and re-layouts, shards(): rows_flat = rows_in.reshape(wide_count * route_cap, model_width)  19 us
    dot_general x3, matrix products, shards(): jnp.dot(rows_flat, w_gate[0], preferred_element_type=jnp.float32)  14 us
  transfers between devices with their start and end apart: 9, of which 6 were waited for; matrix products, arithmetic and copies ran while one was open for 17% of the time, Pallas kernels for 0%

commit v1 on v0

v1 whole, which is shorter than its diff:
```python
import jax
import jax.numpy as jnp
from jax import lax
from jax.experimental import pallas as pl
from jax.experimental.pallas import tpu as pltpu
from jax.sharding import PartitionSpec as P

MESH = pl.DeviceIdType.MESH
BF = jnp.bfloat16
F32 = jnp.float32
SCALE = 192.0 ** (-0.5)
MASKED = -1e30
HALF = 3584
QUART = 1792
CAP = 9


def offsets(j):
    a, b, far = j % 4, (j // 4) % 4, j // 16
    return (a + b + far) % 2, (a + b) % 4, a


def kernel(
    q_hbm, new_hbm, cache_hbm, tok_hbm, ids_ref, gate_ref, table, wg_hbm, wu_hbm, wd_hbm,
    attn_out, moe_out, back,
    cache_v, q_v, new_v, ctx_v, tokh_v, tokq_v, dest_v, mixw_v,
    same_v, other_v, x_v, wg_v, wu_v, wd_v, s_v, sib_v, p_v, got_v, acc_v,
    load_sem, wload_sem, wsend_sem, wrecv_sem, qsend_sem, qrecv_sem, nsend_sem, nrecv_sem,
    csend_sem, crecv_sem, dsend_sem, drecv_sem, ssend_sem, srecv_sem, psend_sem, precv_sem,
    self_sem, got_sem,
):
    w = lax.axis_index("wide")
    t = lax.axis_index("tp")
    xl, z, y = w // 16, (w // 4) % 4, w % 4
    h, c = t // 2, t % 2
    x = 2 * h + xl
    xnext, xprev = (x + 1) % 4, (x + 3) % 4
    sibling = (w, h * 2 + 1 - c)

    def wide_of(far, zz, yy):
        return ((xl + far) % 2) * 16 + ((z + zz) % 4) * 4 + (y + yy) % 4

    loads = [
        pltpu.make_async_copy(tok_hbm.at[:, pl.ds(pl.multiple_of(c * HALF, 128), HALF)], tokh_v, load_sem.at[0]),
        pltpu.make_async_copy(
            tok_hbm.at[:, pl.ds(pl.multiple_of(c * HALF + h * QUART, 128), QUART)], tokq_v, load_sem.at[1]
        ),
        pltpu.make_async_copy(cache_hbm, cache_v, load_sem.at[2]),
        pltpu.make_async_copy(q_hbm.at[w], q_v.at[0], load_sem.at[3]),
        pltpu.make_async_copy(new_hbm.at[w], new_v.at[0], load_sem.at[4]),
    ]
    for load in loads:
        load.start()
    mine = pl.ds(pl.multiple_of(c * HALF, 128), HALF)
    theirs = pl.ds(pl.multiple_of((1 - c) * HALF, 128), HALF)
    hidden_rows = pl.ds(pl.multiple_of(c * 256, 256), 256)
    wloads = [
        pltpu.make_async_copy(wg_hbm.at[mine], wg_v.at[c], wload_sem.at[0]),
        pltpu.make_async_copy(wu_hbm.at[mine], wu_v.at[c], wload_sem.at[1]),
        pltpu.make_async_copy(wd_hbm, wd_v.at[hidden_rows], wload_sem.at[2]),
    ]
    for load in wloads:
        load.start()

    barrier = pltpu.get_barrier_semaphore()

    def greet(i, carry):
        n = (w * 4 + t + i) % 128
        pl.semaphore_signal(barrier, inc=1, device_id=(n // 4, n % 4), device_id_type=MESH)
        return carry

    lax.fori_loop(1, 128, greet, 0)
    pl.semaphore_wait(barrier, 127)

    def remote(src, dst, send, recv, dev):
        return pltpu.make_async_remote_copy(
            src_ref=src, dst_ref=dst, send_sem=send, recv_sem=recv, device_id=dev, device_id_type=MESH
        )

    def send_query(j, carry):
        far, zz, yy = offsets(j)
        n = wide_of(far, zz, yy)
        remote(q_hbm.at[n], q_v.at[j], qsend_sem, qrecv_sem, (n, t)).start()
        remote(new_hbm.at[n], new_v.at[j], nsend_sem, nrecv_sem, (n, t)).start()
        return carry

    lax.fori_loop(1, 32, send_query, 0)

    swaps = [
        remote(wg_hbm.at[theirs], wg_v.at[c], wsend_sem.at[0], wrecv_sem.at[0], sibling),
        remote(wu_hbm.at[theirs], wu_v.at[c], wsend_sem.at[1], wrecv_sem.at[1], sibling),
        remote(wd_hbm, wd_v.at[hidden_rows], wsend_sem.at[2], wrecv_sem.at[2], sibling),
    ]
    for swap in swaps:
        swap.start()

    expert = lax.broadcasted_iota(jnp.int32, (32, 96), 0)
    token = lax.broadcasted_iota(jnp.int32, (32, 96), 1)
    hits = jnp.zeros((32, 96), F32)
    mixw = jnp.zeros((32, 96), F32)
    for k in range(8):
        equal = expert == ids_ref[k : k + 1, :]
        hits = jnp.where(equal, 1.0, hits)
        mixw = jnp.where(equal, gate_ref[k : k + 1, :], mixw)
    first = lax.broadcasted_iota(jnp.int32, (96, 96), 0)
    later = lax.broadcasted_iota(jnp.int32, (96, 96), 1)
    before = ((first // 32 == later // 32) & (first < later)).astype(F32)
    rank = jnp.dot(hits, before, preferred_element_type=F32)
    place = (token // 32).astype(F32) * CAP + rank
    dest_v[...] = jnp.where(hits > 0.0, place, -1.0)
    mixw_v[...] = mixw

    row_id = lax.broadcasted_iota(jnp.int32, (32, 96), 0).astype(F32)

    loads[0].wait()
    loads[1].wait()

    def send_tokens(k, carry):
        def pick(far):
            parts = []
            for a in range(4):
                e = wide_of(far, a + k, a)
                parts.append(jnp.where(row_id == dest_v[pl.ds(e, 1), :], 1.0, 0.0))
            return jnp.concatenate(parts, axis=0).astype(BF)

        base = pl.multiple_of(k * 128, 128)
        for part in range(2):
            cols = slice(part * QUART, (part + 1) * QUART)
            rows = jnp.dot(pick(0), tokh_v[:, cols], preferred_element_type=F32).astype(BF)
            same_v[pl.ds(base, 128), cols] = rows

            @pl.when(k == 0)
            def _():
                x_v[0:32, cols] = rows[0:32]

        other_v[pl.ds(base, 128), :] = jnp.dot(pick(1), tokq_v[...], preferred_element_type=F32).astype(BF)
        for rb in range(2):
            for a in range(4):
                src = pl.ds(pl.multiple_of(k * 128 + a * 32 + rb * 16, 16), 16)
                near = pl.ds(pl.multiple_of(k * 256 + a * 32 + rb * 16, 16), 16)
                away = pl.ds(pl.multiple_of(k * 256 + 128 + a * 32 + rb * 16, 16), 16)

                def send_same():
                    for part in range(2):
                        cols = pl.ds(part * QUART, QUART)
                        remote(
                            same_v.at[src, cols], x_v.at[near, cols], dsend_sem.at[0], drecv_sem.at[k],
                            (wide_of(0, a + k, a), t),
                        ).start()

                if a == 0:
                    pl.when(k > 0)(send_same)
                else:
                    send_same()
                cols = pl.ds(pl.multiple_of(h * QUART, 128), QUART)
                for i, chip in enumerate((xnext, xprev)):
                    remote(
                        other_v.at[src], x_v.at[away, cols], dsend_sem.at[1 + i], drecv_sem.at[k],
                        (wide_of(1, a + k, a), (chip // 2) * 2 + c),
                    ).start()
        return carry

    lax.fori_loop(0, 4, send_tokens, 0)

    for load in loads[2:]:
        load.wait()
    pltpu.make_async_copy(q_v.at[pl.ds(1, 31)], q_v.at[pl.ds(1, 31)], qrecv_sem).wait()
    pltpu.make_async_copy(new_v.at[pl.ds(1, 31)], new_v.at[pl.ds(1, 31)], nrecv_sem).wait()

    def attend(j, carry):
        far, zz, yy = offsets(j)
        o = wide_of(far, 4 - zz, 4 - yy)
        held = table[o]
        length = table[32 + o]
        latents = cache_v[held]
        query = q_v[j]
        packed = new_v[j]
        r16 = lax.broadcasted_iota(jnp.int32, (16, 16), 0)
        c16 = lax.broadcasted_iota(jnp.int32, (16, 16), 1)
        pieces = [
            jnp.dot(
                jnp.where((c16 == r16 * 5 + i) & (r16 < 3), 1.0, 0.0).astype(BF), packed,
                preferred_element_type=F32,
            ).astype(BF)
            for i in range(5)
        ]
        fresh_key = jnp.concatenate(pieces[:4], axis=1)
        nt = (((1,), (1,)), ((), ()))
        scores = lax.dot_general(query, latents, nt, preferred_element_type=F32) * SCALE
        fresh = lax.dot_general(query[:, :512], fresh_key, nt, preferred_element_type=F32)
        fresh += lax.dot_general(query[:, 512:], pieces[4][:, :64], nt, preferred_element_type=F32)
        fresh = fresh * SCALE
        valid = lax.broadcasted_iota(jnp.int32, (48, 256), 1) < length
        step = lax.broadcasted_iota(jnp.int32, (48, 16), 0) // 16
        fresh_valid = lax.broadcasted_iota(jnp.int32, (48, 16), 1) <= step
        scores = jnp.where(valid, scores, MASKED)
        fresh = jnp.where(fresh_valid, fresh, MASKED)
        top = jnp.maximum(
            jnp.max(scores, axis=1, keepdims=True), jnp.max(fresh, axis=1, keepdims=True)
        )
        weights = jnp.where(valid, jnp.exp(scores - top), 0.0)
        fresh_weights = jnp.where(fresh_valid, jnp.exp(fresh - top), 0.0)
        total = jnp.sum(weights, axis=1, keepdims=True) + jnp.sum(fresh_weights, axis=1, keepdims=True)
        context = jnp.dot(weights.astype(BF), latents[:, :512], preferred_element_type=F32)
        context += jnp.dot(fresh_weights.astype(BF), fresh_key, preferred_element_type=F32)
        ctx_v[j] = (context / total).astype(BF)

        @pl.when(j == 0)
        def _():
            pltpu.make_async_copy(ctx_v.at[j], attn_out.at[w], self_sem).start()

        @pl.when(j > 0)
        def _():
            remote(ctx_v.at[j], attn_out.at[w], csend_sem, crecv_sem, (o, t)).start()

        return carry

    lax.fori_loop(0, 32, attend, 0)

    for load in wloads:
        load.wait()
    for swap in swaps:
        swap.wait()

    def swap_sums(k):
        theirs = pl.ds(pl.multiple_of((1 - c) * 128, 128), 128)
        return remote(s_v.at[k, theirs], sib_v.at[k], ssend_sem.at[k], srecv_sem.at[k], sibling)

    def first_half(k):
        @pl.when(k == 0)
        def _():
            part = x_v.at[pl.ds(32, 224)]
            pltpu.make_async_copy(part, part, drecv_sem.at[k]).wait()

        @pl.when(k > 0)
        def _():
            part = x_v.at[pl.ds(pl.multiple_of(k * 256, 256), 256)]
            pltpu.make_async_copy(part, part, drecv_sem.at[k]).wait()

        rows = pl.ds(pl.multiple_of(k * 256, 256), 256)
        for core in range(2):
            for i, weight in enumerate((wg_v, wu_v)):
                col = core * 512 + i * 256
                s_v[k, :, col : col + 256] = jnp.dot(x_v[rows, :], weight[core], preferred_element_type=F32)
        swap_sums(k).start()

    def p_wait(k):
        part = p_v.at[k % 2]
        pltpu.make_async_copy(part, part, psend_sem.at[k % 2]).wait()

    def second_half(k):
        swap_sums(k).wait_recv()

        @pl.when(k >= 2)
        def _():
            p_wait(k)

        own = pl.ds(pl.multiple_of(c * 128, 128), 128)
        hidden = []
        for core in range(2):
            col = core * 512
            gate = s_v[k, own, col : col + 256] + sib_v[k, :, col : col + 256]
            up = s_v[k, own, col + 256 : col + 512] + sib_v[k, :, col + 256 : col + 512]
            hidden.append((gate / (1.0 + jnp.exp(-gate)) * up).astype(BF))
        hidden = jnp.concatenate(hidden, axis=1)
        for q in range(4):
            cols = slice(q * QUART, (q + 1) * QUART)
            p_v[k % 2, :, cols] = jnp.dot(hidden, wd_v[:, cols], preferred_element_type=F32).astype(BF)
        for q in range(4):
            for rb in range(2):
                for a in range(4):
                    n = wide_of(c, 8 - a - k, 4 - a)
                    slot = ((k * 4 + a) * 2 + c) * 2 + h
                    src = p_v.at[k % 2, pl.ds(a * 32 + rb * 16, 16), pl.ds(q * QUART, QUART)]
                    dst = back.at[slot, pl.ds(rb * 16, 16)]

                    def away():
                        remote(src, dst, psend_sem.at[k % 2], precv_sem.at[k], (n, q)).start()

                    if a > 0:
                        away()
                    else:
                        home = (k == 0) & (c == 0) & (h * 2 == q)

                        @pl.when(home)
                        def _():
                            pltpu.make_async_copy(src, dst, psend_sem.at[k % 2]).start()

                        pl.when(jnp.logical_not(home))(away)

    def expert_step(k, carry):
        @pl.when(k < 4)
        def _():
            first_half(k)

        @pl.when(k > 0)
        def _():
            second_half(k - 1)

        return carry

    lax.fori_loop(0, 5, expert_step, 0)

    acc_v[...] = jnp.zeros_like(acc_v)

    def mix(k, carry):
        @pl.when((k == 0) & (c == 0))
        def _():
            part = back.at[pl.ds(0, 15)]
            pltpu.make_async_copy(part, part, precv_sem.at[k]).wait()

        @pl.when((k > 0) | (c == 1))
        def _():
            part = back.at[pl.ds(0, 16)]
            pltpu.make_async_copy(part, part, precv_sem.at[k]).wait()

        fetch = pltpu.make_async_copy(back.at[pl.ds(k * 16, 16)], got_v, got_sem)
        fetch.start()
        parts = []
        for a in range(4):
            for far in range(2):
                e = wide_of(far, a + k, a)
                part = jnp.where(row_id == dest_v[pl.ds(e, 1), :], mixw_v[pl.ds(e, 1), :], 0.0)
                parts += [part, part]
        weights = jnp.concatenate(parts, axis=0)
        high = weights.astype(BF)
        low = (weights - high.astype(F32)).astype(BF)
        fetch.wait()
        rows = got_v[...].reshape(512, QUART)
        tn = (((0,), (0,)), ((), ()))
        acc_v[...] += lax.dot_general(high, rows, tn, preferred_element_type=F32) + lax.dot_general(
            low, rows, tn, preferred_element_type=F32
        )
        return carry

    lax.fori_loop(0, 4, mix, 0)
    moe_out[...] = acc_v[...].astype(BF)

    part = q_v.at[pl.ds(1, 31)]
    pltpu.make_async_copy(part, part, qsend_sem).wait()
    part = new_v.at[pl.ds(1, 31)]
    pltpu.make_async_copy(part, part, nsend_sem).wait()
    part = ctx_v.at[pl.ds(1, 31)]
    pltpu.make_async_copy(part, part, csend_sem).wait()
    pltpu.make_async_copy(part, part, crecv_sem).wait()
    pltpu.make_async_copy(ctx_v.at[0], attn_out.at[w], self_sem).wait()
    part = same_v.at[pl.ds(32, 480)]
    pltpu.make_async_copy(part, part, dsend_sem.at[0]).wait()
    for i in range(2):
        pltpu.make_async_copy(other_v, other_v, dsend_sem.at[1 + i]).wait()
    for k in range(4):
        swap_sums(k).wait_send()
    for k in range(2, 4):
        p_wait(k)


def shards(
    cache, queries, new_latent, cache_len, owner, moe_tokens, expert_ids, gate_weights, w_gate, w_up, w_down
):
    wide = lax.axis_index("wide")
    mine = lax.dynamic_slice_in_dim(owner, wide * 32, 32, 0)
    lengths = lax.dynamic_slice_in_dim(cache_len, wide * 32, 32, 0)
    served = mine[None, :] == jnp.arange(32, dtype=jnp.int32)[:, None]
    held = jnp.sum(jnp.where(served, jnp.arange(32, dtype=jnp.int32)[None, :], 0), axis=1)
    length = jnp.sum(jnp.where(served, lengths[None, :], 0), axis=1)
    table = jnp.concatenate([held, length])
    packed = jnp.pad(new_latent[0], ((0, 0), (0, 0), (0, 64))).reshape(32, 15, 128)
    packed = jnp.pad(packed, ((0, 0), (0, 1), (0, 0)))
    ids = expert_ids.transpose(2, 0, 1).reshape(8, 96)
    gates = gate_weights.transpose(2, 0, 1).reshape(8, 96)

    hbm = pl.BlockSpec(memory_space=pl.ANY)
    vmem = pl.BlockSpec(memory_space=pltpu.VMEM)
    dma = pltpu.SemaphoreType.DMA
    attn, moe, _ = pl.pallas_call(
        kernel,
        out_shape=(
            jax.ShapeDtypeStruct((32, 48, 512), BF),
            jax.ShapeDtypeStruct((96, QUART), BF),
            jax.ShapeDtypeStruct((64, 32, QUART), BF),
        ),
        in_specs=[hbm, hbm, hbm, hbm, vmem, vmem, pl.BlockSpec(memory_space=pltpu.SMEM), hbm, hbm, hbm],
        out_specs=(hbm, vmem, hbm),
        scratch_shapes=[
            pltpu.VMEM((32, 256, 576), BF),
            pltpu.VMEM((32, 48, 576), BF),
            pltpu.VMEM((32, 16, 128), BF),
            pltpu.VMEM((32, 48, 512), BF),
            pltpu.VMEM((96, HALF), BF),
            pltpu.VMEM((96, QUART), BF),
            pltpu.VMEM((32, 96), F32),
            pltpu.VMEM((32, 96), F32),
            pltpu.VMEM((512, HALF), BF),
            pltpu.VMEM((512, QUART), BF),
            pltpu.VMEM((1024, HALF), BF),
            pltpu.VMEM((2, HALF, 256), BF),
            pltpu.VMEM((2, HALF, 256), BF),
            pltpu.VMEM((512, 7168), BF),
            pltpu.VMEM((4, 256, 1024), F32),
            pltpu.VMEM((4, 128, 1024), F32),
            pltpu.VMEM((2, 128, 7168), BF),
            pltpu.VMEM((16, 32, QUART), BF),
            pltpu.VMEM((96, QUART), F32),
            dma((5,)), dma((3,)), dma((3,)), dma((3,)), dma, dma, dma, dma,
            dma, dma, dma((3,)), dma((4,)), dma((4,)), dma((4,)), dma((2,)), dma((4,)),
            dma, dma,
        ],
        compiler_params=pltpu.CompilerParams(
            collective_id=0, has_side_effects=True, vmem_limit_bytes=63 * 1024 * 1024
        ),
        cost_estimate=pl.CostEstimate(flops=13_000_000_000, bytes_accessed=60_000_000, transcendentals=2_000_000),
        name="handover_attend_experts",
    )(
        queries[0].reshape(32, 48, 576), packed, cache, moe_tokens.reshape(96, 7168), ids, gates, table,
        w_gate[0], w_up[0], w_down[0],
    )
    return attn.reshape(1, 32, 3, 16, 512), moe.reshape(3, 32, QUART)


def solution(mesh):
    in_specs = (
        P("wide", None, None),
        P("wide", None, None, "tp", None),
        P("wide", None, None, None),
        P(),
        P(),
        P(None, "wide", None),
        P(None, "wide", None),
        P(None, "wide", None),
        P("wide", None, "tp"),
        P("wide", None, "tp"),
        P("wide", "tp", None),
    )
    out_specs = (P("wide", None, None, "tp", None), P(None, "wide", "tp"))
    return jax.shard_map(shards, mesh=mesh, in_specs=in_specs, out_specs=out_specs, check_vma=False)
```

time: 658 us -> 285 us (0.43)
  the two profiles are of different devices: /device:TPU:15 before, /device:TPU:69 now
where the time goes in v1:
time: 285 us; the launch traced here: 284 us
  Pallas kernels  258 us (91%)
  local copies, waits for them, and re-layouts  24.9 us (9%)
    pallas_call x1, Pallas kernels, shards(): pl.pallas_call(kernel, out_shape=(jax.ShapeDtypeStruct((32, 48, 512), BF)...  258 us
    unnamed x4, local copies, waits for them, and re-layouts  19.8 us

profile of v1, /device:TPU:69, one launch (start us, length us, event | category | flops | bytes accessed | tf_op | source)
XLA Modules:
  0.0 284.1 jit_solution(1233486691045569178)
XLA Ops:
  0.6 0.8 dynamic_slice.7
  1.4 0.8 dynamic_slice.6
  2.2 0.1 select_reduce_fusion.1
  2.3 0.6 pad_add_fusion.table
  2.9 0.7 copy.22
  3.6 0.7 reshape.26.ids_ref
  4.3 0.7 copy.23
  5.0 0.7 reshape.27.gate_ref
  5.6 1.0 copy.25
  6.6 0.1 pad.8.clone
  6.7 0.1 reshape.24
  6.8 0.7 pad.9.new_hbm
  7.5 14.4 %copy.24.cache_hbm = bf16[32,256,576]{2,1,0:T(8,128)(2,1)} copy(bf16[32,256,576]{1,2,0:T(8,128)(2,1)} %param.11) | data formatting | bytes 18874368 | tf_op args[0]
  21.9 257.8 %handover_attend_experts.1 = (bf16[32,48,512]{2,1,0:T(8,128)(2,1)}, bf16[96,1792]{1,0:T(8,128)(2,1)}, bf16[64,32,1792]{2,1,0:T(8,128)(2,1)}) custom-call(bf16[32,48,576]{2,1,0:T(8,128)(2,1)} %bitcast.18, bf16[32,16,128]{2,1,0:T(8,128)(2,1)} %pad.9.new_hbm, bf16[32,256,576]{2,1,0:T(8,128)(2,1)} %copy.24.cache_hbm, bf16[96,7168]{1,0:T(8,128)(2,1)} %bitcast.19, ...), custom_call_target="tpu_custom_call" | custom-call | flops 12999999488 | bytes 60000000 | tf_op jit(solution)/shard_map/handover_attend_experts/pallas_call | solution.py:375
  279.7 2.7 copy.28
  282.4 1.7 copy.29

commit v2 on v1

v2 whole, which is shorter than its diff:
```python
import jax
import jax.numpy as jnp
from jax import lax
from jax.experimental import pallas as pl
from jax.experimental.pallas import tpu as pltpu
from jax.sharding import PartitionSpec as P

MESH = pl.DeviceIdType.MESH
BF = jnp.bfloat16
F32 = jnp.float32
SCALE = 192.0 ** (-0.5)
MASKED = -1e30
HALF = 3584
QUART = 1792
CAP = 9
ROWS = 27
PACK = 112


def offsets(j):
    a, b, far = j % 4, (j // 4) % 4, j // 16
    return (a + b + far) % 2, (a + b) % 4, a


def kernel(
    q_hbm, new_hbm, cache_hbm, tok_hbm, ids_ref, gate_ref, table, wg_hbm, wu_hbm, wd_hbm,
    attn_out, moe_out,
    cache_v, q_v, new_v, ctx_v, tokh_v, tokq_v, dest_v, mixw_v,
    same_v, other_v, x_v, wg_v, wu_v, wd_v, s_v, sib_v, half_v, back_v, acc_v,
    load_sem, wload_sem, wsend_sem, wrecv_sem, qsend_sem, qrecv_sem, nsend_sem, nrecv_sem,
    csend_sem, crecv_sem, dsend_sem, drecv_sem, ssend_sem, srecv_sem, psend_sem, hrecv_sem, near_sem,
    ysend_sem, yrecv_sem, self_sem,
):
    w = lax.axis_index("wide")
    t = lax.axis_index("tp")
    xl, z, y = w // 16, (w // 4) % 4, w % 4
    h, c = t // 2, t % 2
    x = 2 * h + xl
    xnext, xprev = (x + 1) % 4, (x + 3) % 4
    sibling = (w, h * 2 + 1 - c)

    def wide_of(far, zz, yy):
        return ((xl + far) % 2) * 16 + ((z + zz) % 4) * 4 + (y + yy) % 4

    loads = [
        pltpu.make_async_copy(tok_hbm.at[:, pl.ds(pl.multiple_of(c * HALF, 128), HALF)], tokh_v, load_sem.at[0]),
        pltpu.make_async_copy(
            tok_hbm.at[:, pl.ds(pl.multiple_of(c * HALF + h * QUART, 128), QUART)], tokq_v, load_sem.at[1]
        ),
        pltpu.make_async_copy(cache_hbm, cache_v, load_sem.at[2]),
        pltpu.make_async_copy(q_hbm.at[w], q_v.at[0], load_sem.at[3]),
        pltpu.make_async_copy(new_hbm.at[w], new_v.at[0], load_sem.at[4]),
    ]
    for load in loads:
        load.start()
    mine = pl.ds(pl.multiple_of(c * HALF, 128), HALF)
    theirs = pl.ds(pl.multiple_of((1 - c) * HALF, 128), HALF)
    hidden_rows = pl.ds(pl.multiple_of(c * 256, 256), 256)
    wloads = [
        pltpu.make_async_copy(wg_hbm.at[mine], wg_v.at[c], wload_sem.at[0]),
        pltpu.make_async_copy(wu_hbm.at[mine], wu_v.at[c], wload_sem.at[1]),
        pltpu.make_async_copy(wd_hbm, wd_v.at[hidden_rows], wload_sem.at[2]),
    ]
    for load in wloads:
        load.start()

    barrier = pltpu.get_barrier_semaphore()

    def greet(i, carry):
        n = (w * 4 + t + i) % 128
        pl.semaphore_signal(barrier, inc=1, device_id=(n // 4, n % 4), device_id_type=MESH)
        return carry

    lax.fori_loop(1, 128, greet, 0)

    expert = lax.broadcasted_iota(jnp.int32, (32, 96), 0)
    token = lax.broadcasted_iota(jnp.int32, (32, 96), 1)
    hits = jnp.zeros((32, 96), F32)
    mixw = jnp.zeros((32, 96), F32)
    for k in range(8):
        equal = expert == ids_ref[k : k + 1, :]
        hits = jnp.where(equal, 1.0, hits)
        mixw = jnp.where(equal, gate_ref[k : k + 1, :], mixw)
    first = lax.broadcasted_iota(jnp.int32, (96, 96), 0)
    later = lax.broadcasted_iota(jnp.int32, (96, 96), 1)
    before = ((first // 32 == later // 32) & (first < later)).astype(F32)
    rank = jnp.dot(hits, before, preferred_element_type=F32)
    place = (token // 32).astype(F32) * CAP + rank
    dest_v[...] = jnp.where(hits > 0.0, place, -1.0)
    mixw_v[...] = mixw
    row_id = lax.broadcasted_iota(jnp.int32, (32, 96), 0).astype(F32)

    packed_id = lax.broadcasted_iota(jnp.int32, (PACK, 128), 0)
    padded_id = lax.broadcasted_iota(jnp.int32, (PACK, 128), 1)
    pack = (packed_id == (padded_id // 32) * ROWS + padded_id % 32) & (padded_id % 32 < ROWS)
    pack = jnp.where(pack, 1.0, 0.0).astype(BF)

    pl.semaphore_wait(barrier, 127)

    def remote(src, dst, send, recv, dev):
        return pltpu.make_async_remote_copy(
            src_ref=src, dst_ref=dst, send_sem=send, recv_sem=recv, device_id=dev, device_id_type=MESH
        )

    def send_tokens(k):
        def pick(far):
            parts = []
            for a in range(4):
                e = wide_of(far, a + k, a)
                parts.append(jnp.where(row_id == dest_v[pl.ds(e, 1), :], 1.0, 0.0))
            return jnp.concatenate(parts, axis=0).astype(BF)

        picked = pick(0)
        for part in range(2):
            rows = jnp.dot(
                picked, tokh_v[:, part * QUART : (part + 1) * QUART], preferred_element_type=F32
            ).astype(BF)
            for i in range(7):
                same_v[k, part * 7 + i] = rows[:, i * 256 : (i + 1) * 256]

        @pl.when(k == 0)
        def _():
            for i in range(14):
                x_v[0, i, 0:32, :] = same_v[0, i, 0:32, :]

        rows = jnp.dot(pick(1), tokq_v[...], preferred_element_type=F32).astype(BF)
        for i in range(7):
            other_v[k, i] = rows[:, i * 256 : (i + 1) * 256]
        for low, many in ((0, 4), (4, 3)):
            for a in range(4):
                src = pl.ds(a * 32, 32)
                away = pl.ds(128 + a * 32, 32)

                def send_same():
                    for part in range(2):
                        blocks = pl.ds(part * 7 + low, many)
                        remote(
                            same_v.at[k, blocks, src], x_v.at[k, blocks, src], dsend_sem.at[0], drecv_sem.at[k],
                            (wide_of(0, a + k, a), t),
                        ).start()

                if a == 0:
                    pl.when(k > 0)(send_same)
                else:
                    send_same()
                for i, chip in enumerate((xnext, xprev)):
                    remote(
                        other_v.at[k, pl.ds(low, many), src], x_v.at[k, pl.ds(h * 7 + low, many), away],
                        dsend_sem.at[1 + i], drecv_sem.at[k],
                        (wide_of(1, a + k, a), (chip // 2) * 2 + c),
                    ).start()

    loads[0].wait()
    loads[1].wait()
    send_tokens(0)

    swaps = [
        remote(wg_hbm.at[theirs], wg_v.at[c], wsend_sem.at[0], wrecv_sem.at[0], sibling),
        remote(wu_hbm.at[theirs], wu_v.at[c], wsend_sem.at[1], wrecv_sem.at[1], sibling),
        remote(wd_hbm, wd_v.at[hidden_rows], wsend_sem.at[2], wrecv_sem.at[2], sibling),
    ]
    for swap in swaps:
        swap.start()

    def send_query(j, carry):
        far, zz, yy = offsets(j)
        n = wide_of(far, zz, yy)
        remote(q_hbm.at[n], q_v.at[j], qsend_sem, qrecv_sem, (n, t)).start()
        remote(new_hbm.at[n], new_v.at[j], nsend_sem, nrecv_sem, (n, t)).start()
        return carry

    lax.fori_loop(1, 32, send_query, 0)
    send_tokens(1)

    for load in loads[2:]:
        load.wait()
    for load in wloads:
        load.wait()
    for swap in swaps:
        swap.wait()

    def attend(j, carry):
        far, zz, yy = offsets(j)
        o = wide_of(far, 4 - zz, 4 - yy)
        held = table[o]
        length = table[32 + o]
        latents = cache_v[held]
        query = q_v[j]
        packed = new_v[j]
        r16 = lax.broadcasted_iota(jnp.int32, (16, 16), 0)
        c16 = lax.broadcasted_iota(jnp.int32, (16, 16), 1)
        pieces = [
            jnp.dot(
                jnp.where((c16 == r16 * 5 + i) & (r16 < 3), 1.0, 0.0).astype(BF), packed,
                preferred_element_type=F32,
            ).astype(BF)
            for i in range(5)
        ]
        fresh_key = jnp.concatenate(pieces[:4], axis=1)
        nt = (((1,), (1,)), ((), ()))
        scores = jnp.dot(query, latents, preferred_element_type=F32) * SCALE
        fresh = lax.dot_general(query[:, :512], fresh_key, nt, preferred_element_type=F32)
        fresh += lax.dot_general(query[:, 512:], pieces[4][:, :64], nt, preferred_element_type=F32)
        fresh = fresh * SCALE
        valid = lax.broadcasted_iota(jnp.int32, (48, 256), 1) < length
        step = lax.broadcasted_iota(jnp.int32, (48, 16), 0) // 16
        fresh_valid = lax.broadcasted_iota(jnp.int32, (48, 16), 1) <= step
        scores = jnp.where(valid, scores, MASKED)
        fresh = jnp.where(fresh_valid, fresh, MASKED)
        top = jnp.maximum(
            jnp.max(scores, axis=1, keepdims=True), jnp.max(fresh, axis=1, keepdims=True)
        )
        weights = jnp.where(valid, jnp.exp(scores - top), 0.0)
        fresh_weights = jnp.where(fresh_valid, jnp.exp(fresh - top), 0.0)
        total = jnp.sum(weights, axis=1, keepdims=True) + jnp.sum(fresh_weights, axis=1, keepdims=True)
        context = lax.dot_general(weights.astype(BF), latents[:512, :], nt, preferred_element_type=F32)
        context += jnp.dot(fresh_weights.astype(BF), fresh_key, preferred_element_type=F32)
        ctx_v[j] = (context / total).astype(BF)

        @pl.when(j == 0)
        def _():
            pltpu.make_async_copy(ctx_v.at[j], attn_out.at[w], self_sem).start()

        @pl.when(j > 0)
        def _():
            remote(ctx_v.at[j], attn_out.at[w], csend_sem, crecv_sem, (o, t)).start()

        return carry

    def swap_sums(k):
        theirs = pl.ds(pl.multiple_of((1 - c) * 128, 128), 128)
        return remote(s_v.at[k, theirs], sib_v.at[k], ssend_sem.at[k], srecv_sem.at[k], sibling)

    def gate_and_up(k):
        @pl.when(k == 0)
        def _():
            part = x_v.at[k, :, pl.ds(32, 224)]
            pltpu.make_async_copy(part, part, drecv_sem.at[k]).wait()

        @pl.when(k > 0)
        def _():
            part = x_v.at[k]
            pltpu.make_async_copy(part, part, drecv_sem.at[k]).wait()

        rows = jnp.concatenate([x_v[k, i] for i in range(14)], axis=1)
        for core in range(2):
            for i, weight in enumerate((wg_v, wu_v)):
                col = core * 512 + i * 256
                s_v[k, :, col : col + 256] = jnp.dot(rows, weight[core], preferred_element_type=F32)
        swap_sums(k).start()

    def down(k):
        swap_sums(k).wait_recv()
        own = pl.ds(pl.multiple_of(c * 128, 128), 128)
        hidden = []
        for core in range(2):
            col = core * 512
            gate = s_v[k, own, col : col + 256] + sib_v[k, :, col : col + 256]
            up = s_v[k, own, col + 256 : col + 512] + sib_v[k, :, col + 256 : col + 512]
            hidden.append((gate / (1.0 + jnp.exp(-gate)) * up).astype(BF))
        hidden = jnp.concatenate(hidden, axis=1)
        hidden = jnp.dot(pack, hidden, preferred_element_type=F32).astype(BF)
        for i in range(28):
            x_v[k, i % 14, (i // 14) * 128 : (i // 14) * 128 + PACK, :] = jnp.dot(
                hidden, wd_v[:, i * 256 : (i + 1) * 256], preferred_element_type=F32
            ).astype(BF)

        def block(tq, i):
            n = tq * 7 + i
            return x_v.at[k, n % 14, pl.ds(pl.multiple_of((n // 14) * 128, 128), PACK)]

        @pl.when(c == 0)
        def _():
            for i in range(7):
                for core in range(2):
                    tq = 2 * (1 - h) + core
                    remote(
                        block(tq, i), half_v.at[k, 1, i], psend_sem.at[k], hrecv_sem.at[k], (w, tq)
                    ).start()
                pltpu.make_async_copy(block(2 * h, i), half_v.at[k, 0, i], psend_sem.at[k]).start()
                remote(
                    block(2 * h + 1, i), half_v.at[k, 0, i], psend_sem.at[k], near_sem.at[k], sibling
                ).start()

        @pl.when(c == 1)
        def _():
            for i in range(7):
                for tq in (0, 2, 1, 3):
                    remote(
                        block(tq, i), half_v.at[k, 2 + h, i], psend_sem.at[k], hrecv_sem.at[k],
                        (wide_of(1, 0, 0), tq),
                    ).start()

    def finish(k):
        part = x_v.at[k, :, pl.ds(0, 2 * PACK)]
        pltpu.make_async_copy(part, part, psend_sem.at[k]).wait()
        part = half_v.at[k, pl.ds(1, 3)]
        pltpu.make_async_copy(part, part, hrecv_sem.at[k]).wait()

        @pl.when(c == 1)
        def _():
            part = half_v.at[k, 0]
            pltpu.make_async_copy(part, part, near_sem.at[k]).wait()

        tn = (((0,), (0,)), ((), ()))
        for far in range(2):
            for i in range(7):
                both = half_v[k, 2 * far, i].astype(F32) + half_v[k, 2 * far + 1, i].astype(F32)
                x_v[k, far * 7 + i, 0:128, :] = lax.dot_general(
                    pack, both.astype(BF), tn, preferred_element_type=F32
                ).astype(BF)
        for low, many in ((0, 4), (4, 3), (7, 4), (11, 3)):
            for a in range(4):
                n = wide_of(0, 8 - a - k, 4 - a)
                src = x_v.at[k, pl.ds(low, many), pl.ds(a * 32, 32)]
                dst = back_v.at[k * 4 + a, pl.ds(low, many)]

                def away():
                    remote(src, dst, ysend_sem.at[k], yrecv_sem.at[k], (n, t)).start()

                if a > 0:
                    away()
                else:
                    @pl.when(k == 0)
                    def _():
                        pltpu.make_async_copy(src, dst, ysend_sem.at[k]).start()

                    pl.when(k > 0)(away)

    def expert_step(k, carry):
        @pl.when(k < 4)
        def _():
            gate_and_up(k)

        @pl.when(k < 2)
        def _():
            send_tokens(k + 2)

        @pl.when(k < 4)
        def _():
            down(k)

        @pl.when(k == 0)
        def _():
            part = q_v.at[pl.ds(1, 31)]
            pltpu.make_async_copy(part, part, qrecv_sem).wait()
            part = new_v.at[pl.ds(1, 31)]
            pltpu.make_async_copy(part, part, nrecv_sem).wait()

        @pl.when(k > 0)
        def _():
            finish(k - 1)

        @pl.when(k < 4)
        def _():
            lax.fori_loop(k * 8, k * 8 + 8, attend, 0)

        return carry

    lax.fori_loop(0, 5, expert_step, 0)

    acc_v[...] = jnp.zeros_like(acc_v)

    def mix(k, carry):
        part = x_v.at[k, :, pl.ds(0, 128)]
        pltpu.make_async_copy(part, part, ysend_sem.at[k]).wait()

        @pl.when(k == 0)
        def _():
            part = back_v.at[pl.ds(1, 3)]
            pltpu.make_async_copy(part, part, yrecv_sem.at[k]).wait()

        @pl.when(k > 0)
        def _():
            part = back_v.at[pl.ds(k * 4, 4)]
            pltpu.make_async_copy(part, part, yrecv_sem.at[k]).wait()

        parts = []
        for far in range(2):
            for a in range(4):
                e = wide_of(far, a + k, a)
                parts.append(jnp.where(row_id == dest_v[pl.ds(e, 1), :], mixw_v[pl.ds(e, 1), :], 0.0))
        weights = jnp.concatenate(parts, axis=0)
        high = weights.astype(BF)
        low = (weights - high.astype(F32)).astype(BF)
        tn = (((0,), (0,)), ((), ()))
        for i in range(7):
            rows = jnp.concatenate([back_v[k * 4 + a, far * 7 + i] for far in range(2) for a in range(4)], axis=0)
            acc_v[:, i * 256 : (i + 1) * 256] += lax.dot_general(
                high, rows, tn, preferred_element_type=F32
            ) + lax.dot_general(low, rows, tn, preferred_element_type=F32)
        return carry

    lax.fori_loop(0, 4, mix, 0)
    moe_out[...] = acc_v[...].astype(BF)

    part = q_v.at[pl.ds(1, 31)]
    pltpu.make_async_copy(part, part, qsend_sem).wait()
    part = new_v.at[pl.ds(1, 31)]
    pltpu.make_async_copy(part, part, nsend_sem).wait()
    part = ctx_v.at[pl.ds(1, 31)]
    pltpu.make_async_copy(part, part, csend_sem).wait()
    pltpu.make_async_copy(part, part, crecv_sem).wait()
    pltpu.make_async_copy(ctx_v.at[0], attn_out.at[w], self_sem).wait()
    part = x_v.at[pl.ds(0, 3), :, pl.ds(0, 160)]
    pltpu.make_async_copy(part, part, dsend_sem.at[0]).wait()
    for i in range(2):
        pltpu.make_async_copy(other_v, other_v, dsend_sem.at[1 + i]).wait()
    for k in range(4):
        swap_sums(k).wait_send()


def shards(
    cache, queries, new_latent, cache_len, owner, moe_tokens, expert_ids, gate_weights, w_gate, w_up, w_down
):
    wide = lax.axis_index("wide")
    mine = lax.dynamic_slice_in_dim(owner, wide * 32, 32, 0)
    lengths = lax.dynamic_slice_in_dim(cache_len, wide * 32, 32, 0)
    served = mine[None, :] == jnp.arange(32, dtype=jnp.int32)[:, None]
    held = jnp.sum(jnp.where(served, jnp.arange(32, dtype=jnp.int32)[None, :], 0), axis=1)
    length = jnp.sum(jnp.where(served, lengths[None, :], 0), axis=1)
    table = jnp.concatenate([held, length])
    packed = jnp.pad(new_latent[0], ((0, 0), (0, 0), (0, 64))).reshape(32, 15, 128)
    packed = jnp.pad(packed, ((0, 0), (0, 1), (0, 0)))
    ids = expert_ids.transpose(2, 0, 1).reshape(8, 96)
    gates = gate_weights.transpose(2, 0, 1).reshape(8, 96)

    hbm = pl.BlockSpec(memory_space=pl.ANY)
    vmem = pl.BlockSpec(memory_space=pltpu.VMEM)
    dma = pltpu.SemaphoreType.DMA
    attn, moe = pl.pallas_call(
        kernel,
        out_shape=(
            jax.ShapeDtypeStruct((32, 48, 512), BF),
            jax.ShapeDtypeStruct((96, QUART), BF),
        ),
        in_specs=[hbm, hbm, hbm, hbm, vmem, vmem, pl.BlockSpec(memory_space=pltpu.SMEM), hbm, hbm, hbm],
        out_specs=(hbm, vmem),
        scratch_shapes=[
            pltpu.VMEM((32, 576, 256), BF),
            pltpu.VMEM((32, 48, 576), BF),
            pltpu.VMEM((32, 16, 128), BF),
            pltpu.VMEM((32, 48, 512), BF),
            pltpu.VMEM((96, HALF), BF),
            pltpu.VMEM((96, QUART), BF),
            pltpu.VMEM((32, 96), F32),
            pltpu.VMEM((32, 96), F32),
            pltpu.VMEM((4, 14, 128, 256), BF),
            pltpu.VMEM((4, 7, 128, 256), BF),
            pltpu.VMEM((4, 14, 256, 256), BF),
            pltpu.VMEM((2, HALF, 256), BF),
            pltpu.VMEM((2, HALF, 256), BF),
            pltpu.VMEM((512, 7168), BF),
            pltpu.VMEM((4, 256, 1024), F32),
            pltpu.VMEM((4, 128, 1024), F32),
            pltpu.VMEM((4, 4, 7, PACK, 256), BF),
            pltpu.VMEM((16, 14, 32, 256), BF),
            pltpu.VMEM((96, QUART), F32),
            dma((5,)), dma((3,)), dma((3,)), dma((3,)), dma, dma, dma, dma,
            dma, dma, dma((3,)), dma((4,)), dma((4,)), dma((4,)), dma((4,)), dma((4,)), dma((4,)),
            dma((4,)), dma((4,)), dma,
        ],
        compiler_params=pltpu.CompilerParams(
            collective_id=0, has_side_effects=True, vmem_limit_bytes=63 * 1024 * 1024
        ),
        cost_estimate=pl.CostEstimate(flops=13_000_000_000, bytes_accessed=60_000_000, transcendentals=2_000_000),
        name="handover_attend_experts",
    )(
        queries[0].reshape(32, 48, 576), packed, cache.transpose(0, 2, 1), moe_tokens.reshape(96, 7168), ids, gates, table,
        w_gate[0], w_up[0], w_down[0],
    )
    return attn.reshape(1, 32, 3, 16, 512), moe.reshape(3, 32, QUART)


def solution(mesh):
    in_specs = (
        P("wide", None, None),
        P("wide", None, None, "tp", None),
        P("wide", None, None, None),
        P(),
        P(),
        P(None, "wide", None),
        P(None, "wide", None),
        P(None, "wide", None),
        P("wide", None, "tp"),
        P("wide", None, "tp"),
        P("wide", "tp", None),
    )
    out_specs = (P("wide", None, None, "tp", None), P(None, "wide", "tp"))
    return jax.shard_map(shards, mesh=mesh, in_specs=in_specs, out_specs=out_specs, check_vma=False)
```

time: 285 us -> 209 us (0.73)
  the two profiles are of different devices: /device:TPU:69 before, /device:TPU:15 now
where the time goes in v2:
time: 209 us
  Pallas kernels  197 us (94%)
  local copies, waits for them, and re-layouts  10.5 us (5%)
    pallas_call x1, Pallas kernels, shards(): pl.pallas_call(kernel, out_shape=(jax.ShapeDtypeStruct((32, 48, 512), BF)...  197 us
    unnamed x3, local copies, waits for them, and re-layouts  5.39 us

profile of v2, /device:TPU:15, one launch (start us, length us, event | category | flops | bytes accessed | tf_op | source)
XLA Modules:
  0.0 208.7 jit_solution(13211252495520419257)
XLA Ops:
  0.6 0.8 dynamic_slice.7
  1.4 0.8 dynamic_slice.6
  2.2 0.1 select_reduce_fusion.1
  2.3 0.6 pad_add_fusion.table
  2.9 0.7 copy.20
  3.6 0.7 reshape.26.ids_ref
  4.3 0.7 copy.21
  5.0 0.7 reshape.27.gate_ref
  5.6 1.0 copy.22
  6.6 0.1 pad.8.clone
  6.7 0.1 reshape.24
  6.8 0.7 pad.9.new_hbm
  7.5 196.8 %handover_attend_experts.1 = (bf16[32,48,512]{2,1,0:T(8,128)(2,1)}, bf16[96,1792]{1,0:T(8,128)(2,1)}) custom-call(bf16[32,48,576]{2,1,0:T(8,128)(2,1)} %bitcast.20, bf16[32,16,128]{2,1,0:T(8,128)(2,1)} %pad.9.new_hbm, bf16[32,576,256]{2,1,0:T(8,128)(2,1)} %bitcast.16, bf16[96,7168]{1,0:T(8,128)(2,1)} %bitcast.21, s32[8,96]{1,0:T(8,128)} %reshape.26.ids_ref, ...), custom_call_target="tpu_custom_call" | custom-call | flops 12999999488 | bytes 60000000 | tf_op jit(solution)/shard_map/handover_attend_experts/pallas_call | solution.py:431
  204.3 2.7 %copy.25 = bf16[1,32,3,16,512]{4,3,2,1,0:T(8,128)(2,1)} copy(bf16[1,32,3,16,512]{4,3,2,1,0:T(8,128)(2,1)} %bitcast.11) | data formatting | bytes 3145728
  206.9 1.7 copy.26

commit v3 on v2

--- a/solution.py
+++ b/solution.py
@@ -23,38 +23,33 @@
 
 
 def kernel(
-    q_hbm, new_hbm, cache_hbm, tok_hbm, ids_ref, gate_ref, table, wg_hbm, wu_hbm, wd_hbm,
+    q_hbm, new_hbm, cache_hbm, tok_hbm, ids_ref, gate_ref, owner_ref, length_ref, wg_hbm, wu_hbm, wd_hbm,
     attn_out, moe_out,
-    cache_v, q_v, new_v, ctx_v, tokh_v, tokq_v, dest_v, mixw_v,
+    cache_v, q_v, new_v, ctx_v, tok_v, dest_v, mixw_v, near_v, picks_v,
     same_v, other_v, x_v, wg_v, wu_v, wd_v, s_v, sib_v, half_v, back_v, acc_v,
     load_sem, wload_sem, wsend_sem, wrecv_sem, qsend_sem, qrecv_sem, nsend_sem, nrecv_sem,
-    csend_sem, crecv_sem, dsend_sem, drecv_sem, ssend_sem, srecv_sem, psend_sem, hrecv_sem, near_sem,
+    csend_sem, crecv_sem, gsend_sem, grecv_sem, tsend_sem, trecv_sem, dsend_sem, drecv_sem, ssend_sem, srecv_sem, psend_sem, hrecv_sem, near_sem,
     ysend_sem, yrecv_sem, self_sem,
 ):
     w = lax.axis_index("wide")
     t = lax.axis_index("tp")
     xl, z, y = w // 16, (w // 4) % 4, w % 4
     h, c = t // 2, t % 2
-    x = 2 * h + xl
-    xnext, xprev = (x + 1) % 4, (x + 3) % 4
     sibling = (w, h * 2 + 1 - c)
 
     def wide_of(far, zz, yy):
         return ((xl + far) % 2) * 16 + ((z + zz) % 4) * 4 + (y + yy) % 4
 
+    mine = pl.ds(pl.multiple_of(c * HALF, 128), HALF)
+    theirs = pl.ds(pl.multiple_of((1 - c) * HALF, 128), HALF)
     loads = [
-        pltpu.make_async_copy(tok_hbm.at[:, pl.ds(pl.multiple_of(c * HALF, 128), HALF)], tokh_v, load_sem.at[0]),
-        pltpu.make_async_copy(
-            tok_hbm.at[:, pl.ds(pl.multiple_of(c * HALF + h * QUART, 128), QUART)], tokq_v, load_sem.at[1]
-        ),
-        pltpu.make_async_copy(cache_hbm, cache_v, load_sem.at[2]),
-        pltpu.make_async_copy(q_hbm.at[w], q_v.at[0], load_sem.at[3]),
-        pltpu.make_async_copy(new_hbm.at[w], new_v.at[0], load_sem.at[4]),
+        pltpu.make_async_copy(tok_hbm.at[:, mine], tok_v.at[pl.ds(0, 96)], load_sem.at[0]),
+        pltpu.make_async_copy(cache_hbm, cache_v, load_sem.at[1]),
+        pltpu.make_async_copy(q_hbm.at[w], q_v.at[0], load_sem.at[2]),
+        pltpu.make_async_copy(new_hbm.at[w], new_v.at[0], load_sem.at[3]),
     ]
     for load in loads:
         load.start()
-    mine = pl.ds(pl.multiple_of(c * HALF, 128), HALF)
-    theirs = pl.ds(pl.multiple_of((1 - c) * HALF, 128), HALF)
     hidden_rows = pl.ds(pl.multiple_of(c * 256, 256), 256)
     wloads = [
         pltpu.make_async_copy(wg_hbm.at[mine], wg_v.at[c], wload_sem.at[0]),
@@ -66,27 +61,39 @@
 
     barrier = pltpu.get_barrier_semaphore()
 
-    def greet(i, carry):
-        n = (w * 4 + t + i) % 128
-        pl.semaphore_signal(barrier, inc=1, device_id=(n // 4, n % 4), device_id_type=MESH)
+    def greet(n, tq):
+        pl.semaphore_signal(barrier, inc=1, device_id=(n, tq), device_id_type=MESH)
+
+    def greet_wide(i, carry):
+        greet((w + i) % 32, t)
         return carry
 
-    lax.fori_loop(1, 128, greet, 0)
+    lax.fori_loop(1, 32, greet_wide, 0)
+    for i in range(4):
+        greet(wide_of(1, i, 0), (1 - h) * 2 + c)
+    for i in range(1, 4):
+        greet(wide_of(1, 0, i), (1 - h) * 2 + c)
+        greet(w, (t + i) % 4)
+    for i in range(2):
+        greet(wide_of(1, 0, 0), i * 2 + 1 - c)
 
     expert = lax.broadcasted_iota(jnp.int32, (32, 96), 0)
     token = lax.broadcasted_iota(jnp.int32, (32, 96), 1)
     hits = jnp.zeros((32, 96), F32)
     mixw = jnp.zeros((32, 96), F32)
+    ids = jnp.concatenate([ids_ref[i] for i in range(3)], axis=1)
+    gates = jnp.concatenate([gate_ref[i] for i in range(3)], axis=1)
     for k in range(8):
-        equal = expert == ids_ref[k : k + 1, :]
+        equal = expert == ids[k : k + 1, :]
         hits = jnp.where(equal, 1.0, hits)
-        mixw = jnp.where(equal, gate_ref[k : k + 1, :], mixw)
+        mixw = jnp.where(equal, gates[k : k + 1, :], mixw)
     first = lax.broadcasted_iota(jnp.int32, (96, 96), 0)
     later = lax.broadcasted_iota(jnp.int32, (96, 96), 1)
     before = ((first // 32 == later // 32) & (first < later)).astype(F32)
     rank = jnp.dot(hits, before, preferred_element_type=F32)
     place = (token // 32).astype(F32) * CAP + rank
     dest_v[...] = jnp.where(hits > 0.0, place, -1.0)
+    near_v[0] = dest_v[...]
     mixw_v[...] = mixw
     row_id = lax.broadcasted_iota(jnp.int32, (32, 96), 0).astype(F32)
 
@@ -95,64 +102,71 @@
     pack = (packed_id == (padded_id // 32) * ROWS + padded_id % 32) & (padded_id % 32 < ROWS)
     pack = jnp.where(pack, 1.0, 0.0).astype(BF)
 
-    pl.semaphore_wait(barrier, 127)
+    pl.semaphore_wait(barrier, 43)
 
     def remote(src, dst, send, recv, dev):
         return pltpu.make_async_remote_copy(
             src_ref=src, dst_ref=dst, send_sem=send, recv_sem=recv, device_id=dev, device_id_type=MESH
         )
 
+    for d in range(1, 4):
+        peer = (wide_of(0, (1 - c) * d, c * d), t)
+        remote(near_v.at[0], near_v.at[d], tsend_sem, trecv_sem, peer).start()
+    for part in range(4):
+        for d in range(1, 4):
+            peer = (wide_of(0, (1 - c) * d, c * d), t)
+            cols = pl.ds(part * 896, 896)
+            remote(
+                tok_hbm.at[:, pl.ds(pl.multiple_of(c * HALF + part * 896, 128), 896)],
+                tok_v.at[pl.ds(d * 96, 96), cols], gsend_sem, grecv_sem, peer,
+            ).start()
+
     def send_tokens(k):
         def pick(far):
             parts = []
             for a in range(4):
-                e = wide_of(far, a + k, a)
-                parts.append(jnp.where(row_id == dest_v[pl.ds(e, 1), :], 1.0, 0.0))
+                e = wide_of(far, c * (a + k), (1 - c) * a)
+                held = (a + (1 - c) * k) % 4
+                rows = lax.broadcasted_iota(jnp.int32, (32, 384), 0).astype(F32)
+                group = lax.broadcasted_iota(jnp.int32, (32, 384), 1) // 96
+                chosen = (rows == picks_v[pl.ds(e, 1), :]) & (group == held)
+                parts.append(jnp.where(chosen, 1.0, 0.0))
             return jnp.concatenate(parts, axis=0).astype(BF)
 
-        picked = pick(0)
-        for part in range(2):
-            rows = jnp.dot(
-                picked, tokh_v[:, part * QUART : (part + 1) * QUART], preferred_element_type=F32
-            ).astype(BF)
-            for i in range(7):
-                same_v[k, part * 7 + i] = rows[:, i * 256 : (i + 1) * 256]
-
-        @pl.when(k == 0)
-        def _():
-            for i in range(14):
-                x_v[0, i, 0:32, :] = same_v[0, i, 0:32, :]
-
-        rows = jnp.dot(pick(1), tokq_v[...], preferred_element_type=F32).astype(BF)
-        for i in range(7):
-            other_v[k, i] = rows[:, i * 256 : (i + 1) * 256]
-        for low, many in ((0, 4), (4, 3)):
+        for far, out in ((0, same_v), (1, other_v)):
+            picked = pick(far)
+            for part in range(2):
+                rows = jnp.dot(
+                    picked, tok_v[:, part * QUART : (part + 1) * QUART], preferred_element_type=F32
+                ).astype(BF)
+                for i in range(7):
+                    out[k, part * 7 + i] = rows[:, i * 256 : (i + 1) * 256]
+
+        home = c * ((4 - k) % 4)
+        kept = pl.ds(pl.multiple_of(home * 32, 32), 32)
+        for i in range(14):
+            x_v[k, i, kept, :] = same_v[k, i, kept, :]
+        for piece in range(5):
+            low, many = piece * 3, 3 if piece < 4 else 2
+            far_low, far_many = ((0, 3), (3, 2), (5, 3), (8, 3), (11, 3))[piece]
+            far_chip = t if piece < 2 else (1 - h) * 2 + c
             for a in range(4):
                 src = pl.ds(a * 32, 32)
                 away = pl.ds(128 + a * 32, 32)
 
-                def send_same():
-                    for part in range(2):
-                        blocks = pl.ds(part * 7 + low, many)
-                        remote(
-                            same_v.at[k, blocks, src], x_v.at[k, blocks, src], dsend_sem.at[0], drecv_sem.at[k],
-                            (wide_of(0, a + k, a), t),
-                        ).start()
-
-                if a == 0:
-                    pl.when(k > 0)(send_same)
-                else:
-                    send_same()
-                for i, chip in enumerate((xnext, xprev)):
+                @pl.when(home != a)
+                def _():
+                    blocks = pl.ds(low, many)
                     remote(
-                        other_v.at[k, pl.ds(low, many), src], x_v.at[k, pl.ds(h * 7 + low, many), away],
-                        dsend_sem.at[1 + i], drecv_sem.at[k],
-                        (wide_of(1, a + k, a), (chip // 2) * 2 + c),
+                        same_v.at[k, blocks, src], x_v.at[k, blocks, src], dsend_sem.at[0], drecv_sem.at[k],
+                        (wide_of(0, c * (a + k), (1 - c) * a), t),
                     ).start()
 
-    loads[0].wait()
-    loads[1].wait()
-    send_tokens(0)
+                blocks = pl.ds(far_low, far_many)
+                remote(
+                    other_v.at[k, blocks, src], x_v.at[k, blocks, away], dsend_sem.at[1], drecv_sem.at[k],
+                    (wide_of(1, c * (a + k), (1 - c) * a), far_chip),
+                ).start()
 
     swaps = [
         remote(wg_hbm.at[theirs], wg_v.at[c], wsend_sem.at[0], wrecv_sem.at[0], sibling),
@@ -169,10 +183,18 @@
         remote(new_hbm.at[n], new_v.at[j], nsend_sem, nrecv_sem, (n, t)).start()
         return carry
 
-    lax.fori_loop(1, 32, send_query, 0)
+    lax.fori_loop(1, 16, send_query, 0)
+    loads[0].wait()
+    part = near_v.at[pl.ds(1, 3)]
+    pltpu.make_async_copy(part, part, trecv_sem).wait()
+    part = tok_v.at[pl.ds(96, 288)]
+    pltpu.make_async_copy(part, part, grecv_sem).wait()
+    picks_v[...] = jnp.concatenate([near_v[i] for i in range(4)], axis=1)
+    send_tokens(0)
+    lax.fori_loop(16, 32, send_query, 0)
     send_tokens(1)
 
-    for load in loads[2:]:
+    for load in loads[1:]:
         load.wait()
     for load in wloads:
         load.wait()
@@ -182,8 +204,12 @@
     def attend(j, carry):
         far, zz, yy = offsets(j)
         o = wide_of(far, 4 - zz, 4 - yy)
-        held = table[o]
-        length = table[32 + o]
+
+        def find(r, found):
+            return jnp.where(owner_ref[w * 32 + r] == o, r, found)
+
+        held = lax.fori_loop(0, 32, find, 0)
+        length = length_ref[w * 32 + held]
         latents = cache_v[held]
         query = q_v[j]
         packed = new_v[j]
@@ -229,24 +255,21 @@
 
     def swap_sums(k):
         theirs = pl.ds(pl.multiple_of((1 - c) * 128, 128), 128)
-        return remote(s_v.at[k, theirs], sib_v.at[k], ssend_sem.at[k], srecv_sem.at[k], sibling)
+        return remote(s_v.at[k % 2, theirs], sib_v.at[k], ssend_sem.at[k % 2], srecv_sem.at[k], sibling)
 
     def gate_and_up(k):
-        @pl.when(k == 0)
-        def _():
-            part = x_v.at[k, :, pl.ds(32, 224)]
-            pltpu.make_async_copy(part, part, drecv_sem.at[k]).wait()
-
-        @pl.when(k > 0)
-        def _():
-            part = x_v.at[k]
-            pltpu.make_async_copy(part, part, drecv_sem.at[k]).wait()
+        part = x_v.at[k, :, pl.ds(0, 224)]
+        pltpu.make_async_copy(part, part, drecv_sem.at[k]).wait()
+
+        @pl.when(k >= 2)
+        def _():
+            swap_sums(k).wait_send()
 
         rows = jnp.concatenate([x_v[k, i] for i in range(14)], axis=1)
         for core in range(2):
             for i, weight in enumerate((wg_v, wu_v)):
                 col = core * 512 + i * 256
-                s_v[k, :, col : col + 256] = jnp.dot(rows, weight[core], preferred_element_type=F32)
+                s_v[k % 2, :, col : col + 256] = jnp.dot(rows, weight[core], preferred_element_type=F32)
         swap_sums(k).start()
 
     def down(k):
@@ -255,8 +278,8 @@
         hidden = []
         for core in range(2):
             col = core * 512
-            gate = s_v[k, own, col : col + 256] + sib_v[k, :, col : col + 256]
-            up = s_v[k, own, col + 256 : col + 512] + sib_v[k, :, col + 256 : col + 512]
+            gate = s_v[k % 2, own, col : col + 256] + sib_v[k, :, col : col + 256]
+            up = s_v[k % 2, own, col + 256 : col + 512] + sib_v[k, :, col + 256 : col + 512]
             hidden.append((gate / (1.0 + jnp.exp(-gate)) * up).astype(BF))
         hidden = jnp.concatenate(hidden, axis=1)
         hidden = jnp.dot(pack, hidden, preferred_element_type=F32).astype(BF)
@@ -402,31 +425,28 @@
     pltpu.make_async_copy(part, part, csend_sem).wait()
     pltpu.make_async_copy(part, part, crecv_sem).wait()
     pltpu.make_async_copy(ctx_v.at[0], attn_out.at[w], self_sem).wait()
-    part = x_v.at[pl.ds(0, 3), :, pl.ds(0, 160)]
+    part = near_v.at[pl.ds(1, 3)]
+    pltpu.make_async_copy(part, part, tsend_sem).wait()
+    part = tok_v.at[pl.ds(96, 288)]
+    pltpu.make_async_copy(part, part, gsend_sem).wait()
+    part = same_v.at[:, :, pl.ds(0, 96)]
     pltpu.make_async_copy(part, part, dsend_sem.at[0]).wait()
-    for i in range(2):
-        pltpu.make_async_copy(other_v, other_v, dsend_sem.at[1 + i]).wait()
-    for k in range(4):
+    pltpu.make_async_copy(other_v, other_v, dsend_sem.at[1]).wait()
+    for k in range(2, 4):
         swap_sums(k).wait_send()
 
 
 def shards(
     cache, queries, new_latent, cache_len, owner, moe_tokens, expert_ids, gate_weights, w_gate, w_up, w_down
 ):
-    wide = lax.axis_index("wide")
-    mine = lax.dynamic_slice_in_dim(owner, wide * 32, 32, 0)
-    lengths = lax.dynamic_slice_in_dim(cache_len, wide * 32, 32, 0)
-    served = mine[None, :] == jnp.arange(32, dtype=jnp.int32)[:, None]
-    held = jnp.sum(jnp.where(served, jnp.arange(32, dtype=jnp.int32)[None, :], 0), axis=1)
-    length = jnp.sum(jnp.where(served, lengths[None, :], 0), axis=1)
-    table = jnp.concatenate([held, length])
     packed = jnp.pad(new_latent[0], ((0, 0), (0, 0), (0, 64))).reshape(32, 15, 128)
     packed = jnp.pad(packed, ((0, 0), (0, 1), (0, 0)))
-    ids = expert_ids.transpose(2, 0, 1).reshape(8, 96)
-    gates = gate_weights.transpose(2, 0, 1).reshape(8, 96)
+    ids = expert_ids.transpose(0, 2, 1)
+    gates = gate_weights.transpose(0, 2, 1)
 
     hbm = pl.BlockSpec(memory_space=pl.ANY)
     vmem = pl.BlockSpec(memory_space=pltpu.VMEM)
+    smem = pl.BlockSpec(memory_space=pltpu.SMEM)
     dma = pltpu.SemaphoreType.DMA
     attn, moe = pl.pallas_call(
         kernel,
@@ -434,39 +454,40 @@
             jax.ShapeDtypeStruct((32, 48, 512), BF),
             jax.ShapeDtypeStruct((96, QUART), BF),
         ),
-        in_specs=[hbm, hbm, hbm, hbm, vmem, vmem, pl.BlockSpec(memory_space=pltpu.SMEM), hbm, hbm, hbm],
+        in_specs=[hbm, hbm, hbm, hbm, vmem, vmem, smem, smem, hbm, hbm, hbm],
         out_specs=(hbm, vmem),
         scratch_shapes=[
             pltpu.VMEM((32, 576, 256), BF),
             pltpu.VMEM((32, 48, 576), BF),
             pltpu.VMEM((32, 16, 128), BF),
             pltpu.VMEM((32, 48, 512), BF),
-            pltpu.VMEM((96, HALF), BF),
-            pltpu.VMEM((96, QUART), BF),
+            pltpu.VMEM((384, HALF), BF),
             pltpu.VMEM((32, 96), F32),
             pltpu.VMEM((32, 96), F32),
+            pltpu.VMEM((4, 32, 96), F32),
+            pltpu.VMEM((32, 384), F32),
             pltpu.VMEM((4, 14, 128, 256), BF),
-            pltpu.VMEM((4, 7, 128, 256), BF),
+            pltpu.VMEM((4, 14, 128, 256), BF),
             pltpu.VMEM((4, 14, 256, 256), BF),
             pltpu.VMEM((2, HALF, 256), BF),
             pltpu.VMEM((2, HALF, 256), BF),
             pltpu.VMEM((512, 7168), BF),
-            pltpu.VMEM((4, 256, 1024), F32),
+            pltpu.VMEM((2, 256, 1024), F32),
             pltpu.VMEM((4, 128, 1024), F32),
             pltpu.VMEM((4, 4, 7, PACK, 256), BF),
             pltpu.VMEM((16, 14, 32, 256), BF),
             pltpu.VMEM((96, QUART), F32),
-            dma((5,)), dma((3,)), dma((3,)), dma((3,)), dma, dma, dma, dma,
-            dma, dma, dma((3,)), dma((4,)), dma((4,)), dma((4,)), dma((4,)), dma((4,)), dma((4,)),
+            dma((4,)), dma((3,)), dma((3,)), dma((3,)), dma, dma, dma, dma,
+            dma, dma, dma, dma, dma, dma, dma((2,)), dma((4,)), dma((2,)), dma((4,)), dma((4,)), dma((4,)), dma((4,)),
             dma((4,)), dma((4,)), dma,
         ],
         compiler_params=pltpu.CompilerParams(
-            collective_id=0, has_side_effects=True, vmem_limit_bytes=63 * 1024 * 1024
+            collective_id=0, has_side_effects=True, vmem_limit_bytes=64 * 1024 * 1024 - 65536
         ),
         cost_estimate=pl.CostEstimate(flops=13_000_000_000, bytes_accessed=60_000_000, transcendentals=2_000_000),
         name="handover_attend_experts",
     )(
-        queries[0].reshape(32, 48, 576), packed, cache.transpose(0, 2, 1), moe_tokens.reshape(96, 7168), ids, gates, table,
+        queries[0].reshape(32, 48, 576), packed, cache.transpose(0, 2, 1), moe_tokens.reshape(96, 7168), ids, gates, owner, cache_len,
         w_gate[0], w_up[0], w_down[0],
     )
     return attn.reshape(1, 32, 3, 16, 512), moe.reshape(3, 32, QUART)

time: 209 us -> 186 us (0.89); the launches traced: 209 us -> 183 us
  Pallas kernels: 197 us -> 176 us
  local copies, waits for them, and re-layouts: 10.5 us -> 6.26 us
    pallas_call x1, Pallas kernels: 197 us -> 176 us  [shards(): pl.pallas_call(kernel, out_shape=(jax.ShapeDtypeStruct((32, 48, 512), BF)...]
where the time goes in v3:
time: 186 us; the launch traced here: 183 us
  Pallas kernels  176 us (95%)
  local copies, waits for them, and re-layouts  6.26 us (3%)
    pallas_call x1, Pallas kernels, shards(): pl.pallas_call(kernel, out_shape=(jax.ShapeDtypeStruct((32, 48, 512), BF)...  176 us
    unnamed x3, local copies, waits for them, and re-layouts  5.39 us

profile of v3, /device:TPU:15, one launch (start us, length us, event | category | flops | bytes accessed | tf_op | source)
XLA Modules:
  0.0 183.3 jit_solution(788335480986413661)
XLA Ops:
  0.6 1.0 copy.15
  1.6 0.1 pad.8.clone
  1.7 0.1 reshape.16
  1.8 0.7 pad.9.new_hbm
  2.5 176.4 %handover_attend_experts.1 = (bf16[32,48,512]{2,1,0:T(8,128)(2,1)}, bf16[96,1792]{1,0:T(8,128)(2,1)}) custom-call(bf16[32,48,576]{2,1,0:T(8,128)(2,1)} %bitcast.18, bf16[32,16,128]{2,1,0:T(8,128)(2,1)} %pad.9.new_hbm, bf16[32,576,256]{2,1,0:T(8,128)(2,1)} %bitcast.14, bf16[96,7168]{1,0:T(8,128)(2,1)} %bitcast.19, s32[3,8,32]{2,1,0:T(8,128)} %bitcast.20, ...), custom_call_target="tpu_custom_call" | custom-call | flops 12999999488 | bytes 60000000 | tf_op jit(solution)/shard_map/handover_attend_experts/pallas_call | solution.py:451
  178.9 2.7 %copy.18 = bf16[1,32,3,16,512]{4,3,2,1,0:T(8,128)(2,1)} copy(bf16[1,32,3,16,512]{4,3,2,1,0:T(8,128)(2,1)} %bitcast.11) | data formatting | bytes 3145728
  181.5 1.7 copy.19

commit v4 on v3

--- a/solution.py
+++ b/solution.py
@@ -25,7 +25,7 @@
 def kernel(
     q_hbm, new_hbm, cache_hbm, tok_hbm, ids_ref, gate_ref, owner_ref, length_ref, wg_hbm, wu_hbm, wd_hbm,
     attn_out, moe_out,
-    cache_v, q_v, new_v, ctx_v, tok_v, dest_v, mixw_v, near_v, picks_v,
+    cache_v, q_v, new_v, ctx_v, tok_v, dest_v, mixw_v, near_v, picks_v, newin_v, newout_v,
     same_v, other_v, x_v, wg_v, wu_v, wd_v, s_v, sib_v, half_v, back_v, acc_v,
     load_sem, wload_sem, wsend_sem, wrecv_sem, qsend_sem, qrecv_sem, nsend_sem, nrecv_sem,
     csend_sem, crecv_sem, gsend_sem, grecv_sem, tsend_sem, trecv_sem, dsend_sem, drecv_sem, ssend_sem, srecv_sem, psend_sem, hrecv_sem, near_sem,
@@ -46,7 +46,7 @@
         pltpu.make_async_copy(tok_hbm.at[:, mine], tok_v.at[pl.ds(0, 96)], load_sem.at[0]),
         pltpu.make_async_copy(cache_hbm, cache_v, load_sem.at[1]),
         pltpu.make_async_copy(q_hbm.at[w], q_v.at[0], load_sem.at[2]),
-        pltpu.make_async_copy(new_hbm.at[w], new_v.at[0], load_sem.at[3]),
+        pltpu.make_async_copy(new_hbm, newin_v, load_sem.at[3]),
     ]
     for load in loads:
         load.start()
@@ -102,6 +102,24 @@
     pack = (packed_id == (padded_id // 32) * ROWS + padded_id % 32) & (padded_id % 32 < ROWS)
     pack = jnp.where(pack, 1.0, 0.0).astype(BF)
 
+    loads[3].wait()
+    pieces = []
+    for i in range(3):
+        for j in range(5):
+            piece = newin_v[i, :, j * 128 : min(j * 128 + 128, 576)]
+            if j == 4:
+                piece = jnp.concatenate([piece, jnp.zeros((32, 64), BF)], axis=1)
+            pieces.append(piece)
+    to_row = lax.broadcasted_iota(jnp.int32, (512, 480), 0)
+    from_row = lax.broadcasted_iota(jnp.int32, (512, 480), 1)
+    moved = (to_row // 16 == from_row % 32) & (to_row % 16 == from_row // 32)
+    rows = jnp.dot(
+        jnp.where(moved, 1.0, 0.0).astype(BF), jnp.concatenate(pieces, axis=0), preferred_element_type=F32
+    ).astype(BF)
+    for i in range(32):
+        newout_v[i] = rows[i * 16 : i * 16 + 16]
+    new_v[0] = newout_v[w]
+
     pl.semaphore_wait(barrier, 43)
 
     def remote(src, dst, send, recv, dev):
@@ -158,13 +176,13 @@
                 def _():
                     blocks = pl.ds(low, many)
                     remote(
-                        same_v.at[k, blocks, src], x_v.at[k, blocks, src], dsend_sem.at[0], drecv_sem.at[k],
+                        same_v.at[k, blocks, src], x_v.at[k, blocks, src], dsend_sem.at[k], drecv_sem.at[k],
                         (wide_of(0, c * (a + k), (1 - c) * a), t),
                     ).start()
 
                 blocks = pl.ds(far_low, far_many)
                 remote(
-                    other_v.at[k, blocks, src], x_v.at[k, blocks, away], dsend_sem.at[1], drecv_sem.at[k],
+                    other_v.at[k, blocks, src], x_v.at[k, blocks, away], dsend_sem.at[4], drecv_sem.at[k],
                     (wide_of(1, c * (a + k), (1 - c) * a), far_chip),
                 ).start()
 
@@ -180,7 +198,7 @@
         far, zz, yy = offsets(j)
         n = wide_of(far, zz, yy)
         remote(q_hbm.at[n], q_v.at[j], qsend_sem, qrecv_sem, (n, t)).start()
-        remote(new_hbm.at[n], new_v.at[j], nsend_sem, nrecv_sem, (n, t)).start()
+        remote(newout_v.at[n], new_v.at[j], nsend_sem, nrecv_sem, (n, t)).start()
         return carry
 
     lax.fori_loop(1, 16, send_query, 0)
@@ -191,10 +209,10 @@
     pltpu.make_async_copy(part, part, grecv_sem).wait()
     picks_v[...] = jnp.concatenate([near_v[i] for i in range(4)], axis=1)
     send_tokens(0)
+    send_tokens(1)
     lax.fori_loop(16, 32, send_query, 0)
-    send_tokens(1)
-
-    for load in loads[1:]:
+
+    for load in loads[1:3]:
         load.wait()
     for load in wloads:
         load.wait()
@@ -295,14 +313,15 @@
         @pl.when(c == 0)
         def _():
             for i in range(7):
+                p = i // 4
                 for core in range(2):
                     tq = 2 * (1 - h) + core
                     remote(
-                        block(tq, i), half_v.at[k, 1, i], psend_sem.at[k], hrecv_sem.at[k], (w, tq)
+                        block(tq, i), half_v.at[k, 1, i], psend_sem.at[k], hrecv_sem.at[p, k], (w, tq)
                     ).start()
-                pltpu.make_async_copy(block(2 * h, i), half_v.at[k, 0, i], psend_sem.at[k]).start()
+                pltpu.make_async_copy(block(2 * h, i), half_v.at[k, 0, i], near_sem.at[p, k]).start()
                 remote(
-                    block(2 * h + 1, i), half_v.at[k, 0, i], psend_sem.at[k], near_sem.at[k], sibling
+                    block(2 * h + 1, i), half_v.at[k, 0, i], psend_sem.at[k], near_sem.at[p, k], sibling
                 ).start()
 
         @pl.when(c == 1)
@@ -310,33 +329,28 @@
             for i in range(7):
                 for tq in (0, 2, 1, 3):
                     remote(
-                        block(tq, i), half_v.at[k, 2 + h, i], psend_sem.at[k], hrecv_sem.at[k],
+                        block(tq, i), half_v.at[k, 2 + h, i], psend_sem.at[k], hrecv_sem.at[i // 4, k],
                         (wide_of(1, 0, 0), tq),
                     ).start()
 
-    def finish(k):
-        part = x_v.at[k, :, pl.ds(0, 2 * PACK)]
-        pltpu.make_async_copy(part, part, psend_sem.at[k]).wait()
-        part = half_v.at[k, pl.ds(1, 3)]
-        pltpu.make_async_copy(part, part, hrecv_sem.at[k]).wait()
-
-        @pl.when(c == 1)
-        def _():
-            part = half_v.at[k, 0]
-            pltpu.make_async_copy(part, part, near_sem.at[k]).wait()
-
+    def finish(k, low, many, part_id):
+        part = half_v.at[k, pl.ds(1, 3), pl.ds(low, many)]
+        pltpu.make_async_copy(part, part, hrecv_sem.at[part_id, k]).wait()
+        part = half_v.at[k, 0, pl.ds(low, many)]
+        pltpu.make_async_copy(part, part, near_sem.at[part_id, k]).wait()
         tn = (((0,), (0,)), ((), ()))
         for far in range(2):
-            for i in range(7):
+            for i in range(low, low + many):
                 both = half_v[k, 2 * far, i].astype(F32) + half_v[k, 2 * far + 1, i].astype(F32)
-                x_v[k, far * 7 + i, 0:128, :] = lax.dot_general(
+                same_v[k, far * 7 + i] = lax.dot_general(
                     pack, both.astype(BF), tn, preferred_element_type=F32
                 ).astype(BF)
-        for low, many in ((0, 4), (4, 3), (7, 4), (11, 3)):
+        for far in range(2):
             for a in range(4):
                 n = wide_of(0, 8 - a - k, 4 - a)
-                src = x_v.at[k, pl.ds(low, many), pl.ds(a * 32, 32)]
-                dst = back_v.at[k * 4 + a, pl.ds(low, many)]
+                blocks = pl.ds(far * 7 + low, many)
+                src = same_v.at[k, blocks, pl.ds(a * 32, 32)]
+                dst = back_v.at[k * 4 + a, blocks]
 
                 def away():
                     remote(src, dst, ysend_sem.at[k], yrecv_sem.at[k], (n, t)).start()
@@ -372,7 +386,10 @@
 
         @pl.when(k > 0)
         def _():
-            finish(k - 1)
+            part = same_v.at[k - 1, :, pl.ds(0, 96)]
+            pltpu.make_async_copy(part, part, dsend_sem.at[k - 1]).wait()
+            finish(k - 1, 0, 4, 0)
+            finish(k - 1, 4, 3, 1)
 
         @pl.when(k < 4)
         def _():
@@ -385,7 +402,7 @@
     acc_v[...] = jnp.zeros_like(acc_v)
 
     def mix(k, carry):
-        part = x_v.at[k, :, pl.ds(0, 128)]
+        part = same_v.at[k]
         pltpu.make_async_copy(part, part, ysend_sem.at[k]).wait()
 
         @pl.when(k == 0)
@@ -429,18 +446,24 @@
     pltpu.make_async_copy(part, part, tsend_sem).wait()
     part = tok_v.at[pl.ds(96, 288)]
     pltpu.make_async_copy(part, part, gsend_sem).wait()
-    part = same_v.at[:, :, pl.ds(0, 96)]
-    pltpu.make_async_copy(part, part, dsend_sem.at[0]).wait()
-    pltpu.make_async_copy(other_v, other_v, dsend_sem.at[1]).wait()
+    pltpu.make_async_copy(other_v, other_v, dsend_sem.at[4]).wait()
     for k in range(2, 4):
         swap_sums(k).wait_send()
+    for k in range(4):
+        @pl.when(c == 0)
+        def _():
+            part = half_v.at[k, pl.ds(0, 3)]
+            pltpu.make_async_copy(part, part, psend_sem.at[k]).wait()
+
+        @pl.when(c == 1)
+        def _():
+            part = half_v.at[k]
+            pltpu.make_async_copy(part, part, psend_sem.at[k]).wait()
 
 
 def shards(
     cache, queries, new_latent, cache_len, owner, moe_tokens, expert_ids, gate_weights, w_gate, w_up, w_down
 ):
-    packed = jnp.pad(new_latent[0], ((0, 0), (0, 0), (0, 64))).reshape(32, 15, 128)
-    packed = jnp.pad(packed, ((0, 0), (0, 1), (0, 0)))
     ids = expert_ids.transpose(0, 2, 1)
     gates = gate_weights.transpose(0, 2, 1)
 
@@ -466,6 +489,8 @@
             pltpu.VMEM((32, 96), F32),
             pltpu.VMEM((4, 32, 96), F32),
             pltpu.VMEM((32, 384), F32),
+            pltpu.VMEM((3, 32, 576), BF),
+            pltpu.VMEM((32, 16, 128), BF),
             pltpu.VMEM((4, 14, 128, 256), BF),
             pltpu.VMEM((4, 14, 128, 256), BF),
             pltpu.VMEM((4, 14, 256, 256), BF),
@@ -478,7 +503,7 @@
             pltpu.VMEM((16, 14, 32, 256), BF),
             pltpu.VMEM((96, QUART), F32),
             dma((4,)), dma((3,)), dma((3,)), dma((3,)), dma, dma, dma, dma,
-            dma, dma, dma, dma, dma, dma, dma((2,)), dma((4,)), dma((2,)), dma((4,)), dma((4,)), dma((4,)), dma((4,)),
+            dma, dma, dma, dma, dma, dma, dma((5,)), dma((4,)), dma((2,)), dma((4,)), dma((4,)), dma((2, 4)), dma((2, 4)),
             dma((4,)), dma((4,)), dma,
         ],
         compiler_params=pltpu.CompilerParams(
@@ -487,7 +512,7 @@
         cost_estimate=pl.CostEstimate(flops=13_000_000_000, bytes_accessed=60_000_000, transcendentals=2_000_000),
         name="handover_attend_experts",
     )(
-        queries[0].reshape(32, 48, 576), packed, cache.transpose(0, 2, 1), moe_tokens.reshape(96, 7168), ids, gates, owner, cache_len,
+        queries[0].reshape(32, 48, 576), new_latent[0].transpose(1, 0, 2), cache.transpose(0, 2, 1), moe_tokens.reshape(96, 7168), ids, gates, owner, cache_len,
         w_gate[0], w_up[0], w_down[0],
     )
     return attn.reshape(1, 32, 3, 16, 512), moe.reshape(3, 32, QUART)

time: 186 us -> 180 us (0.968)
  Pallas kernels: 176 us -> 173 us
    pallas_call x1, Pallas kernels: 176 us -> 173 us  [shards(): pl.pallas_call(kernel, out_shape=(jax.ShapeDtypeStruct((32, 48, 512), BF)...]
    unnamed x3 -> x2, local copies, waits for them, and re-layouts: 5.39 us -> 4.4 us
where the time goes in v4:
time: 180 us; the launch traced here: 178 us
  Pallas kernels  173 us (96%)
  local copies, waits for them, and re-layouts  4.4 us (2%)
    pallas_call x1, Pallas kernels, shards(): pl.pallas_call(kernel, out_shape=(jax.ShapeDtypeStruct((32, 48, 512), BF)...  173 us
    unnamed x2, local copies, waits for them, and re-layouts  4.4 us

profile of v4, /device:TPU:15, one launch (start us, length us, event | category | flops | bytes accessed | tf_op | source)
XLA Modules:
  0.0 177.9 jit_solution(9227053351430981925)
XLA Ops:
  0.6 172.9 %handover_attend_experts.1 = (bf16[32,48,512]{2,1,0:T(8,128)(2,1)}, bf16[96,1792]{1,0:T(8,128)(2,1)}) custom-call(bf16[32,48,576]{2,1,0:T(8,128)(2,1)} %bitcast.19, bf16[3,32,576]{2,1,0:T(8,128)(2,1)} %bitcast.21, bf16[32,576,256]{2,1,0:T(8,128)(2,1)} %bitcast.15, bf16[96,7168]{1,0:T(8,128)(2,1)} %bitcast.20, s32[3,8,32]{2,1,0:T(8,128)} %bitcast.22, ...), custom_call_target="tpu_custom_call" | custom-call | flops 12999999488 | bytes 60000000 | tf_op jit(solution)/shard_map/handover_attend_experts/pallas_call | solution.py:474
  173.5 2.7 %copy.15 = bf16[1,32,3,16,512]{4,3,2,1,0:T(8,128)(2,1)} copy(bf16[1,32,3,16,512]{4,3,2,1,0:T(8,128)(2,1)} %bitcast.13) | data formatting | bytes 3145728
  176.2 1.7 copy.16

commit v5 on v4

--- a/solution.py
+++ b/solution.py
@@ -15,6 +15,7 @@
 CAP = 9
 ROWS = 27
 PACK = 112
+PART_OF = (0, 0, 1, 1, 2, 2, 3)
 
 
 def offsets(j):
@@ -164,10 +165,10 @@
         kept = pl.ds(pl.multiple_of(home * 32, 32), 32)
         for i in range(14):
             x_v[k, i, kept, :] = same_v[k, i, kept, :]
-        for piece in range(5):
-            low, many = piece * 3, 3 if piece < 4 else 2
-            far_low, far_many = ((0, 3), (3, 2), (5, 3), (8, 3), (11, 3))[piece]
-            far_chip = t if piece < 2 else (1 - h) * 2 + c
+        for piece in range(4):
+            low, many = ((0, 4), (4, 4), (8, 3), (11, 3))[piece]
+            far_low, far_many = ((0, 5), (5, 3), (8, 3), (11, 3))[piece]
+            far_chip = t if piece < 1 else (1 - h) * 2 + c
             for a in range(4):
                 src = pl.ds(a * 32, 32)
                 away = pl.ds(128 + a * 32, 32)
@@ -313,7 +314,7 @@
         @pl.when(c == 0)
         def _():
             for i in range(7):
-                p = i // 4
+                p = PART_OF[i]
                 for core in range(2):
                     tq = 2 * (1 - h) + core
                     remote(
@@ -329,7 +330,7 @@
             for i in range(7):
                 for tq in (0, 2, 1, 3):
                     remote(
-                        block(tq, i), half_v.at[k, 2 + h, i], psend_sem.at[k], hrecv_sem.at[i // 4, k],
+                        block(tq, i), half_v.at[k, 2 + h, i], psend_sem.at[k], hrecv_sem.at[PART_OF[i], k],
                         (wide_of(1, 0, 0), tq),
                     ).start()
 
@@ -388,8 +389,10 @@
         def _():
             part = same_v.at[k - 1, :, pl.ds(0, 96)]
             pltpu.make_async_copy(part, part, dsend_sem.at[k - 1]).wait()
-            finish(k - 1, 0, 4, 0)
-            finish(k - 1, 4, 3, 1)
+            finish(k - 1, 0, 2, 0)
+            finish(k - 1, 2, 2, 1)
+            finish(k - 1, 4, 2, 2)
+            finish(k - 1, 6, 1, 3)
 
         @pl.when(k < 4)
         def _():
@@ -503,7 +506,7 @@
             pltpu.VMEM((16, 14, 32, 256), BF),
             pltpu.VMEM((96, QUART), F32),
             dma((4,)), dma((3,)), dma((3,)), dma((3,)), dma, dma, dma, dma,
-            dma, dma, dma, dma, dma, dma, dma((5,)), dma((4,)), dma((2,)), dma((4,)), dma((4,)), dma((2, 4)), dma((2, 4)),
+            dma, dma, dma, dma, dma, dma, dma((5,)), dma((4,)), dma((2,)), dma((4,)), dma((4,)), dma((4, 4)), dma((4, 4)),
             dma((4,)), dma((4,)), dma,
         ],
         compiler_params=pltpu.CompilerParams(

time: 180 us -> 178 us (0.989)
  Pallas kernels: 173 us -> 170 us
    pallas_call x1, Pallas kernels: 173 us -> 170 us  [shards(): pl.pallas_call(kernel, out_shape=(jax.ShapeDtypeStruct((32, 48, 512), BF)...]
where the time goes in v5:
time: 178 us; the launch traced here: 175 us
  Pallas kernels  170 us (96%)
  local copies, waits for them, and re-layouts  4.4 us (2%)
    pallas_call x1, Pallas kernels, shards(): pl.pallas_call(kernel, out_shape=(jax.ShapeDtypeStruct((32, 48, 512), BF)...  170 us
    unnamed x2, local copies, waits for them, and re-layouts  4.4 us

profile of v5, /device:TPU:15, one launch (start us, length us, event | category | flops | bytes accessed | tf_op | source)
XLA Modules:
  0.0 175.0 jit_solution(10602583476772550062)
XLA Ops:
  0.6 170.0 %handover_attend_experts.1 = (bf16[32,48,512]{2,1,0:T(8,128)(2,1)}, bf16[96,1792]{1,0:T(8,128)(2,1)}) custom-call(bf16[32,48,576]{2,1,0:T(8,128)(2,1)} %bitcast.19, bf16[3,32,576]{2,1,0:T(8,128)(2,1)} %bitcast.21, bf16[32,576,256]{2,1,0:T(8,128)(2,1)} %bitcast.15, bf16[96,7168]{1,0:T(8,128)(2,1)} %bitcast.20, s32[3,8,32]{2,1,0:T(8,128)} %bitcast.22, ...), custom_call_target="tpu_custom_call" | custom-call | flops 12999999488 | bytes 60000000 | tf_op jit(solution)/shard_map/handover_attend_experts/pallas_call | solution.py:477
  170.6 2.7 %copy.15 = bf16[1,32,3,16,512]{4,3,2,1,0:T(8,128)(2,1)} copy(bf16[1,32,3,16,512]{4,3,2,1,0:T(8,128)(2,1)} %bitcast.13) | data formatting | bytes 3145728
  173.3 1.7 copy.16

commit v6 on v5

--- a/solution.py
+++ b/solution.py
@@ -365,43 +365,6 @@
 
                     pl.when(k > 0)(away)
 
-    def expert_step(k, carry):
-        @pl.when(k < 4)
-        def _():
-            gate_and_up(k)
-
-        @pl.when(k < 2)
-        def _():
-            send_tokens(k + 2)
-
-        @pl.when(k < 4)
-        def _():
-            down(k)
-
-        @pl.when(k == 0)
-        def _():
-            part = q_v.at[pl.ds(1, 31)]
-            pltpu.make_async_copy(part, part, qrecv_sem).wait()
-            part = new_v.at[pl.ds(1, 31)]
-            pltpu.make_async_copy(part, part, nrecv_sem).wait()
-
-        @pl.when(k > 0)
-        def _():
-            part = same_v.at[k - 1, :, pl.ds(0, 96)]
-            pltpu.make_async_copy(part, part, dsend_sem.at[k - 1]).wait()
-            finish(k - 1, 0, 2, 0)
-            finish(k - 1, 2, 2, 1)
-            finish(k - 1, 4, 2, 2)
-            finish(k - 1, 6, 1, 3)
-
-        @pl.when(k < 4)
-        def _():
-            lax.fori_loop(k * 8, k * 8 + 8, attend, 0)
-
-        return carry
-
-    lax.fori_loop(0, 5, expert_step, 0)
-
     acc_v[...] = jnp.zeros_like(acc_v)
 
     def mix(k, carry):
@@ -434,7 +397,48 @@
             ) + lax.dot_general(low, rows, tn, preferred_element_type=F32)
         return carry
 
-    lax.fori_loop(0, 4, mix, 0)
+    def expert_step(k, carry):
+        @pl.when(k < 4)
+        def _():
+            gate_and_up(k)
+
+        @pl.when(k < 2)
+        def _():
+            send_tokens(k + 2)
+
+        @pl.when(k < 4)
+        def _():
+            down(k)
+
+        @pl.when(k == 0)
+        def _():
+            part = q_v.at[pl.ds(1, 31)]
+            pltpu.make_async_copy(part, part, qrecv_sem).wait()
+            part = new_v.at[pl.ds(1, 31)]
+            pltpu.make_async_copy(part, part, nrecv_sem).wait()
+
+        @pl.when(k == 4)
+        def _():
+            lax.fori_loop(0, 2, mix, 0)
+
+        @pl.when(k > 0)
+        def _():
+            part = same_v.at[k - 1, :, pl.ds(0, 96)]
+            pltpu.make_async_copy(part, part, dsend_sem.at[k - 1]).wait()
+            finish(k - 1, 0, 2, 0)
+            finish(k - 1, 2, 2, 1)
+            finish(k - 1, 4, 2, 2)
+            finish(k - 1, 6, 1, 3)
+
+        @pl.when(k < 4)
+        def _():
+            lax.fori_loop(k * 8, k * 8 + 8, attend, 0)
+
+        return carry
+
+    lax.fori_loop(0, 5, expert_step, 0)
+
+    lax.fori_loop(2, 4, mix, 0)
     moe_out[...] = acc_v[...].astype(BF)
 
     part = q_v.at[pl.ds(1, 31)]

time: 178 us -> 178 us (level)
  no operation moved by 1% of the time
where the time goes in v6:
time: 178 us; the launch traced here: 175 us
  Pallas kernels  170 us (96%)
  local copies, waits for them, and re-layouts  4.4 us (2%)
    pallas_call x1, Pallas kernels, shards(): pl.pallas_call(kernel, out_shape=(jax.ShapeDtypeStruct((32, 48, 512), BF)...  170 us
    unnamed x2, local copies, waits for them, and re-layouts  4.4 us

profile of v6, /device:TPU:15, one launch (start us, length us, event | category | flops | bytes accessed | tf_op | source)
XLA Modules:
  0.0 175.0 jit_solution(18197442091156738012)
XLA Ops:
  0.6 170.0 %handover_attend_experts.1 = (bf16[32,48,512]{2,1,0:T(8,128)(2,1)}, bf16[96,1792]{1,0:T(8,128)(2,1)}) custom-call(bf16[32,48,576]{2,1,0:T(8,128)(2,1)} %bitcast.19, bf16[3,32,576]{2,1,0:T(8,128)(2,1)} %bitcast.21, bf16[32,576,256]{2,1,0:T(8,128)(2,1)} %bitcast.15, bf16[96,7168]{1,0:T(8,128)(2,1)} %bitcast.20, s32[3,8,32]{2,1,0:T(8,128)} %bitcast.22, ...), custom_call_target="tpu_custom_call" | custom-call | flops 12999999488 | bytes 60000000 | tf_op jit(solution)/shard_map/handover_attend_experts/pallas_call | solution.py:481
  170.6 2.7 %copy.15 = bf16[1,32,3,16,512]{4,3,2,1,0:T(8,128)(2,1)} copy(bf16[1,32,3,16,512]{4,3,2,1,0:T(8,128)(2,1)} %bitcast.13) | data formatting | bytes 3145728
  173.3 1.7 copy.16
